TPU v7x, 256 devices: a whole 4x4x8 slice. The times are simulated.
256 devices in a mesh: seq: 32 (over y, x, core), exp: 8 (over z).
Axes of the slice: x: 4, y: 4, z: 8, core: 2. Of those that a mesh axis runs over, the one named last changes fastest.
Arguments:
- patches: bfloat16 [2, 16384, 4096], P(None, 'seq', 'exp'), may hold values from -32 to 32
- grad_out: bfloat16 [2, 16384, 4096], P(None, 'seq', 'exp'), may hold values from -6 to 6
- phi_t: bfloat16 [16, 4096], P(None, 'exp'), may hold values from -0.0625 to 0.0625
- w_in: bfloat16 [8, 4096, 8192], P('exp', None, 'seq'), may hold values from -0.09375 to 0.09375
- w_out: bfloat16 [8, 8192, 4096], P('exp', 'seq'), may hold values from -0.0625 to 0.0625
Outputs:
- grad_patches: bfloat16 [2, 16384, 4096], P(None, 'seq', 'exp')
- grad_phi: float32 [16, 4096], P(None, 'exp')
- grad_w_in: bfloat16 [8, 4096, 8192], P('exp', None, 'seq')
- grad_w_out: bfloat16 [8, 8192, 4096], P('exp', 'seq')
All inputs are finite; a program needn't handle non-finite values.
Results may differ from a plain program's by a relative error of at most 0.015.
Values may be sent and summed in bfloat16 or wider, within the bound.
A program may use at most 64 MiB of HBM per device.

v0:
```python
import math

import jax
import jax.numpy as jnp
from jax import lax
from jax.sharding import PartitionSpec as P

slope_coef = 0.7978845608
cubic_coef = 0.044715


def gelu_value(value):
    inner = slope_coef * (value + cubic_coef * value * value * value)
    return 0.5 * value * (1.0 + jnp.tanh(inner))


def gelu_slope(value):
    inner = slope_coef * (value + cubic_coef * value * value * value)
    tangent = jnp.tanh(inner)
    return 0.5 * (1.0 + tangent) + 0.5 * value * (1.0 - tangent * tangent) * slope_coef * (
        1.0 + 3.0 * cubic_coef * value * value
    )


def local(patches, grad_out, phi_t, w_in, w_out):
    exp_rank = lax.axis_index("exp")
    width_part = patches.shape[2]
    images = patches.shape[0]
    full_rows, full_phi = (
        lax.all_gather(patches, "exp", axis=2, tiled=True),
        lax.all_gather(phi_t, "exp", axis=1, tiled=True),
    )
    logits = jnp.einsum("ipd,sd->ips", full_rows, full_phi, preferred_element_type=jnp.float32)
    col_peak = lax.pmax(jnp.max(logits, axis=1), "seq")
    col_total = lax.psum(jnp.sum(jnp.exp(logits - col_peak[:, None, :]), axis=1), "seq")
    dispatch = jnp.exp(logits - col_peak[:, None, :]) / col_total[:, None, :]
    combine = jax.nn.softmax(logits, axis=2)
    dispatch_b = dispatch.astype(jnp.bfloat16)
    combine_b = combine.astype(jnp.bfloat16)
    input_part = jnp.einsum("ips,ipd->isd", dispatch_b, patches, preferred_element_type=jnp.float32)
    slot_inputs = lax.psum(input_part, "seq").astype(jnp.bfloat16)
    owner_rows = lax.all_to_all(slot_inputs, "exp", split_axis=1, concat_axis=2, tiled=True)
    full_width = owner_rows.shape[2]
    w_first = w_in[0]
    w_second = w_out[0]
    rows = owner_rows.reshape(-1, full_width)
    hidden_pre = jnp.dot(rows, w_first, preferred_element_type=jnp.float32)
    active = gelu_value(hidden_pre).astype(jnp.bfloat16)
    out_part = jnp.dot(active, w_second, preferred_element_type=jnp.float32).reshape(
        images, -1, full_width
    )
    slot_outputs = lax.psum(out_part, "seq").astype(jnp.bfloat16)
    local_outputs = lax.all_to_all(slot_outputs, "exp", split_axis=2, concat_axis=1, tiled=True)
    comb_part = jnp.einsum(
        "ipd,isd->ips", grad_out, local_outputs, preferred_element_type=jnp.float32
    )
    grad_part = jnp.einsum("ips,ipd->isd", combine_b, grad_out, preferred_element_type=jnp.float32)
    slot_grads = lax.psum(grad_part, "seq").astype(jnp.bfloat16)
    owner_grads = lax.all_to_all(slot_grads, "exp", split_axis=1, concat_axis=2, tiled=True)
    grad_rows = owner_grads.reshape(-1, full_width)
    act_grad = jnp.einsum("sd,fd->sf", grad_rows, w_second, preferred_element_type=jnp.float32)
    pre_grad = (act_grad * gelu_slope(hidden_pre)).astype(jnp.bfloat16)
    grad_w_out = jnp.einsum(
        "sf,sd->fd", active, grad_rows, preferred_element_type=jnp.float32
    ).astype(jnp.bfloat16)[None]
    grad_w_in = jnp.einsum("sd,sf->df", rows, pre_grad, preferred_element_type=jnp.float32).astype(
        jnp.bfloat16
    )[None]
    input_part_grad = jnp.einsum(
        "sf,df->sd", pre_grad, w_first, preferred_element_type=jnp.float32
    ).reshape(images, -1, full_width)
    input_grads = lax.psum(input_part_grad, "seq").astype(jnp.bfloat16)
    all_grads = lax.all_gather(input_grads, "exp", axis=1, tiled=True)
    local_grads = lax.dynamic_slice_in_dim(all_grads, exp_rank * width_part, width_part, 2)
    comb_grad = lax.psum(comb_part, "exp")
    disp_grad = jnp.einsum("ipd,isd->ips", full_rows, all_grads, preferred_element_type=jnp.float32)
    col_dots = lax.psum(jnp.sum(dispatch * disp_grad, axis=1), "seq")
    row_dots = jnp.sum(combine * comb_grad, axis=2, keepdims=True)
    logit_grad = combine * (comb_grad - row_dots) + dispatch * (disp_grad - col_dots[:, None, :])
    logit_b = logit_grad.astype(jnp.bfloat16)
    grad_patches = (
        jnp.einsum("ips,isd->ipd", dispatch_b, local_grads, preferred_element_type=jnp.float32)
        + jnp.einsum("ips,sd->ipd", logit_b, phi_t, preferred_element_type=jnp.float32)
    ).astype(jnp.bfloat16)
    phi_part = jnp.einsum("ips,ipd->sd", logit_b, patches, preferred_element_type=jnp.float32)
    norm_factor = 1.0 / math.sqrt(images * patches.shape[1] * lax.axis_size("seq"))
    grad_phi = lax.psum(phi_part, "seq") * norm_factor
    return (grad_patches, grad_phi, grad_w_in, grad_w_out)


def solution(mesh):
    in_specs = (
        P(None, "seq", "exp"),
        P(None, "seq", "exp"),
        P(None, "exp"),
        P("exp", None, "seq"),
        P("exp", "seq", None),
    )
    out_specs = (
        P(None, "seq", "exp"),
        P(None, "exp"),
        P("exp", None, "seq"),
        P("exp", "seq", None),
    )
    return jax.shard_map(local, mesh=mesh, in_specs=in_specs, out_specs=out_specs, check_vma=False)
```

profile of v0, /device:TPU:1, one launch (start us, length us, event | category | flops | bytes accessed | tf_op | source)
XLA Modules:
  0.0 908.8 jit_solution(16555165495861099579)
XLA Ops:
  7.2 0.0 copy-start
  7.2 0.0 all-gather.2.cloned.1.call-start
  7.2 0.7 all-gather.2.cloned.1.call-update
  7.9 23.8 %all_gather.10 = bf16[16,4096]{1,0:T(8,128)(2,1)S(1)} all-gather(bf16[16,512]{1,0:T(8,128)(2,1)} %param.7), channel_id=1, replica_groups=mesh['seq'=32,'exp'=8] {'exp'}, dimensions={1}, use_global_device_ids=true | all-gather | bytes 147456 | tf_op jit(solution)/shard_map/all_gather | solution.py:31
  31.7 0.0 copy-start.2
  31.7 76.5 %all-gather.2.cloned.1.call-done = bf16[2,512,4096]{2,1,0:T(8,128)(2,1)} async-done(((bf16[2,512,512]{2,1,0:T(8,128)(2,1)}), bf16[2,512,4096]{2,1,0:T(8,128)(2,1)}) %all-gather.2.cloned.1.call-update) | async-done | bytes 8388624 | tf_op jit(solution)/shard_map/all_gather | solution.py:30
  108.2 5.7 fusion.54
  113.9 62.7 %pmax.7 = f32[2,16]{1,0:T(2,128)S(1)} all-reduce(f32[2,16]{1,0:T(2,128)S(1)} %get-tuple-element.10), channel_id=1, replica_groups=mesh['seq'=32,'exp'=8] {'seq'}, use_global_device_ids=true, to_apply=%region_1.0 | all-reduce | flops 32 | bytes 256 | tf_op jit(solution)/shard_map/pmax | solution.py:34
  176.6 0.7 fusion.53
  177.3 0.2 fusion.31
  177.4 67.1 %psum.56 = f32[2,16]{1,0:T(2,128)S(1)} all-reduce(f32[2,16]{1,0:T(2,128)S(1)} %fusion.31), channel_id=1, replica_groups=mesh['seq'=32,'exp'=8] {'seq'}, use_global_device_ids=true, to_apply=%region_3.0 | all-reduce | flops 32 | bytes 256 | tf_op jit(solution)/shard_map/psum | solution.py:35
  244.5 1.5 fusion.38
  246.0 0.0 copy-done.2
  246.0 0.2 fusion.34
  246.3 118.9 %all-reduce.6 = (bf16[2,16,512]{2,1,0:T(8,128)(2,1)S(1)}, bf16[2,16,512]{2,1,0:T(8,128)(2,1)S(1)}) all-reduce(f32[2,16,512]{2,1,0:T(8,128)S(1)} %fusion.34, f32[2,16,512]{2,1,0:T(8,128)S(1)} %fusion.38), channel_id=1, replica_groups=mesh['seq'=32,'exp'=8] {'seq'}, use_global_device_ids=true, to_apply=%region_6.0 | all-reduce | flops 32768 | bytes 196608 | tf_op jit(solution)/shard_map/psum | solution.py:58
  365.2 0.6 copy.15
  365.8 4.0 all-to-all-start.1
  369.8 0.6 copy.13
  370.4 6.2 all-to-all-done.1
  376.6 3.3 all-to-all-start
  380.0 6.7 all-to-all-done
  386.8 0.0 copy-start.1
  386.8 0.0 copy-done
  386.8 0.4 multiply_convert_fusion
  387.2 1.1 copy-done.1
  388.4 0.6 fusion.21
  389.0 0.0 copy-start.7
  389.0 0.6 copy-done.7
  389.6 0.6 fusion.6
  390.3 126.4 %psum.59 = bf16[2,2,4096]{2,1,0:T(2,128)(2,1)S(1)} all-reduce(f32[2,2,4096]{2,1,0:T(2,128)S(1)} %fusion.6), channel_id=1, replica_groups=mesh['seq'=32,'exp'=8] {'seq'}, use_global_device_ids=true, to_apply=%region_8.0 | all-reduce | flops 16384 | bytes 98304 | tf_op jit(solution)/shard_map/psum | solution.py:72
  516.7 18.7 %all_gather.11 = bf16[2,16,4096]{2,0,1:T(2,128)(2,1)S(1)} all-gather(bf16[2,2,4096]{2,0,1:T(2,128)(2,1)S(1)} %copy.17), channel_id=1, replica_groups=mesh['seq'=32,'exp'=8] {'exp'}, dimensions={1}, use_global_device_ids=true | all-gather | bytes 294912 | tf_op jit(solution)/shard_map/all_gather | solution.py:73
  535.4 0.6 dot_general.58
  536.0 2.6 fusion.4
  538.6 0.9 copy.18
  539.5 6.8 multiply_reduce_fusion.1
  546.3 130.5 %all-reduce = (bf16[2,2,4096]{2,1,0:T(2,128)(2,1)S(1)}, f32[2,16]{1,0:T(2,128)S(1)}) all-reduce(f32[2,2,4096]{2,1,0:T(2,128)} %fusion.4, f32[2,16]{1,0:T(2,128)} %get-tuple-element.14), channel_id=1, replica_groups=mesh['seq'=32,'exp'=8] {'seq'}, use_global_device_ids=true, to_apply=%region_9.0 | all-reduce | flops 16416 | bytes 98560 | tf_op jit(solution)/shard_map/psum | solution.py:52
  676.8 3.8 copy.19
  680.6 0.0 copy-start.8
  680.6 4.8 reshape.33
  685.5 3.3 all-to-all-start.2
  688.8 0.2 all-reduce.5.cloned.1.call-start
  689.0 2.7 fusion.32
  691.8 0.0 copy-done.8
  691.8 2.1 fusion.2
  693.8 1.8 all-to-all-done.2
  695.6 5.5 reshape.34
  701.1 4.9 copy.20
  706.0 0.0 copy-start.4
  706.0 0.0 copy-start.5
  706.1 1.0 convolution_bitcast_fusion.1
  707.1 0.0 copy-start.3
  707.1 0.0 copy-start.6
  707.1 0.0 all-reduce.5.cloned.1.call-update
  707.1 2.1 fusion.3
  709.2 64.1 %all-reduce.5.cloned.1.call-done = f32[2,512,16]{1,2,0:T(8,128)} async-done(((f32[2,512,16]{1,2,0:T(8,128)}), f32[2,512,16]{1,2,0:T(8,128)}) %all-reduce.5.cloned.1.call-update) | async-done | bytes 65552 | tf_op jit(solution)/shard_map/psum | solution.py:75
  773.3 0.0 copy-done.4
  773.3 0.0 copy-done.5
  773.3 0.0 copy-done.3
  773.3 1.2 convolution_bitcast_fusion.2
  774.5 123.7 %psum.63 = f32[16,512]{1,0:T(8,128)S(1)} all-reduce(f32[16,512]{1,0:T(8,128)S(1)} %convolution_bitcast_fusion.2), channel_id=1, replica_groups=mesh['seq'=32,'exp'=8] {'seq'}, use_global_device_ids=true, to_apply=%region_14.0 | all-reduce | flops 8192 | bytes 65536 | tf_op jit(solution)/shard_map/psum | solution.py:87
  898.2 0.6 broadcast_multiply_fusion
  898.8 0.0 copy-done.6
  898.8 3.2 add_convert_fusion
  (7 shorter events, 0.1 us)
Async XLA Ops:
  7.2 379.7 %copy-start = (bf16[1,4096,256]{2,1,0:T(8,128)(2,1)S(1)}, bf16[1,4096,256]{2,1,0:T(8,128)(2,1)}, u32[]{:S(2)}) copy-start(bf16[1,4096,256]{2,1,0:T(8,128)(2,1)} %param.8) | copy-start | bytes 6291460
  7.2 101.0 %all-gather.2.cloned.1.call-start = ((), (), s32[]{:S(2)}) async-start(), calls=%async_computation.3 | async-start | bytes 9437184 | tf_op jit(solution)/shard_map/all_gather | solution.py:30
  31.7 214.3 %copy-start.2 = (bf16[2,512,512]{2,1,0:T(8,128)(2,1)S(1)}, bf16[2,512,512]{2,1,0:T(8,128)(2,1)}, u32[]{:S(2)}) copy-start(bf16[2,512,512]{2,1,0:T(8,128)(2,1)} %param.6) | copy-start | bytes 3145732
  365.8 10.8 %all-to-all-start.1 = ((bf16[2,16,512]{2,0,1:T(2,128)(2,1)}), bf16[2,16,512]{2,0,1:T(2,128)(2,1)S(1)}, u32[]{:S(2)}, u32[]{:S(2)}) async-start(bf16[2,16,512]{2,0,1:T(2,128)(2,1)} %copy.15), calls=%async_computation.1 | async-start | bytes 65536 | tf_op jit(solution)/shard_map/all_to_all | solution.py:42
  376.6 10.1 %all-to-all-start = ((bf16[2,16,512]{2,0,1:T(2,128)(2,1)}), bf16[2,16,512]{2,0,1:T(2,128)(2,1)S(1)}, u32[]{:S(2)}, u32[]{:S(2)}) async-start(bf16[2,16,512]{2,0,1:T(2,128)(2,1)} %copy.13), calls=%async_computation | async-start | bytes 65536 | tf_op jit(solution)/shard_map/all_to_all | solution.py:59
  386.8 1.6 copy-start.1
  389.0 0.6 copy-start.7
  680.6 11.1 %copy-start.8 = (bf16[4,256]{1,0:T(4,128)(2,1)S(1)}, bf16[4,256]{1,0:T(4,128)(2,1)}, u32[]{:S(2)}) copy-start(bf16[4,256]{1,0:T(4,128)(2,1)} %copy-done.7) | copy-start | bytes 6148
  685.5 10.1 %all-to-all-start.2 = ((bf16[8,2,1024]{2,1,0:T(2,128)(2,1)}), bf16[8,2,1024]{2,1,0:T(2,128)(2,1)S(1)}, u32[]{:S(2)}, u32[]{:S(2)}) async-start(bf16[8,2,1024]{2,1,0:T(2,128)(2,1)} %reshape.33), calls=%async_computation.2 | async-start | bytes 65536 | tf_op jit(solution)/shard_map/all_to_all | solution.py:53
  688.8 84.5 %all-reduce.5.cloned.1.call-start = ((), (), s32[]{:S(2)}) async-start(), calls=%async_computation.4 | async-start | bytes 131072 | tf_op jit(solution)/shard_map/psum | solution.py:75
  706.0 67.2 %copy-start.4 = (f32[2,512,16]{1,2,0:T(8,128)S(1)}, f32[2,512,16]{1,2,0:T(8,128)}, u32[]{:S(2)}) copy-start(f32[2,512,16]{1,2,0:T(8,128)} %get-tuple-element.15) | copy-start | bytes 196612
  706.0 67.2 %copy-start.5 = (f32[2,512,16]{1,2,0:T(8,128)S(1)}, f32[2,512,16]{1,2,0:T(8,128)}, u32[]{:S(2)}) copy-start(f32[2,512,16]{1,2,0:T(8,128)} %get-tuple-element.9) | copy-start | bytes 196612
  707.1 66.2 %copy-start.3 = (bf16[2,512,512]{2,1,0:T(8,128)(2,1)S(1)}, bf16[2,512,512]{2,1,0:T(8,128)(2,1)}, u32[]{:S(2)}) copy-start(bf16[2,512,512]{2,1,0:T(8,128)(2,1)} %param.5) | copy-start | bytes 3145732
  707.1 191.7 %copy-start.6 = (bf16[16,512]{1,0:T(8,128)(2,1)S(1)}, bf16[16,512]{1,0:T(8,128)(2,1)}, u32[]{:S(2)}) copy-start(bf16[16,512]{1,0:T(8,128)(2,1)} %param.7) | copy-start | bytes 49156
Sparse Core Ops, SparseCore 0:
  9.8 98.3 all-gather.1
  707.3 65.9 all-reduce.4
where the time goes:
time: 913 us; the launch traced here: 909 us
  blocking collectives  672 us (74%)
  waiting for transfers between devices  156 us (17%)
  matrix products  30.9 us (3%)
  local copies, waits for them, and re-layouts  23.7 us (3%)
  between operations  14.2 us (2%)
  starting transfers between devices  10.9 us (1%)
    psum x1, blocking collectives, local(): slot_outputs = lax.psum(out_part, 'seq').astype(jnp.bfloat16)  131 us
    psum x1, blocking collectives, local(): input_grads = lax.psum(input_part_grad, 'seq').astype(jnp.bfloat16)  126 us
    psum x1, blocking collectives, local(): grad_phi = lax.psum(phi_part, 'seq') * norm_factor  124 us
    psum x1, blocking collectives, local(): slot_grads = lax.psum(grad_part, 'seq').astype(jnp.bfloat16)  119 us
    all_gather x1, waiting for transfers between devices, local(): lax.all_gather(patches, 'exp', axis=2, tiled=True)  76.5 us
    psum x1, blocking collectives, local(): lax.psum(jnp.sum(jnp.exp(logits - col_peak[:, None, :]), axis=1), 'seq')  67.1 us
    psum x1, waiting for transfers between devices, local(): comb_grad = lax.psum(comb_part, 'exp')  64.1 us
    pmax x1, blocking collectives, local(): col_peak = lax.pmax(jnp.max(logits, axis=1), 'seq')  62.7 us
  transfers between devices with their start and end apart: 5, of which 5 were waited for; matrix products, arithmetic and copies ran while one was open for 1% of the time, Pallas kernels for 0%

commit v1 on v0

v1 whole, which is shorter than its diff:
```python
import math

import jax
import jax.numpy as jnp
from jax import lax
from jax.experimental import pallas as pl
from jax.experimental.pallas import tpu as pltpu
from jax.sharding import PartitionSpec as P

MESH = pl.DeviceIdType.MESH
F32 = jnp.float32
BF16 = jnp.bfloat16

slope_coef = 0.7978845608
cubic_coef = 0.044715

NS = 32
NZ = 8
LANE = 128


def nn(a, b):
    return lax.dot_general(a, b, (((1,), (0,)), ((), ())), preferred_element_type=F32)


def nt(a, b):
    return lax.dot_general(a, b, (((1,), (1,)), ((), ())), preferred_element_type=F32)


def tn(a, b):
    return lax.dot_general(a, b, (((0,), (0,)), ((), ())), preferred_element_type=F32)


def iota(shape, dim):
    return lax.broadcasted_iota(jnp.int32, shape, dim)


def kernel(
    patches, grad_out, phi_t, w_in, w_out,
    grad_patches, grad_phi, grad_w_in, grad_w_out,
    pv, gv, phv, wiv, wov, gpv, gphv, gwiv, gwov,
    asend, arecv, logit, csend, crecv, dtmp, dsend, drecv, rows_f,
    esend, erecv, fsend, frecv, lse_b, gsend, grecv, hbuf, isend, irecv, jbuf,
    in_sem, out_sem, send_sem, recv_sem,
):
    r = lax.axis_index("seq")
    z = lax.axis_index("exp")
    owner = lax.rem(r, 16) // 2
    q = (r // 16) * 2 + lax.rem(r, 2)

    def tile_of(rr):
        return (lax.rem(rr, 16) // 2) * 4 + (rr // 16) * 2 + lax.rem(rr, 2)

    loads = [
        pltpu.make_async_copy(src, dst, in_sem.at[k])
        for k, (src, dst) in enumerate(
            [(phi_t, phv), (patches, pv), (grad_out, gv), (w_in, wiv), (w_out, wov)]
        )
    ]
    for load in loads:
        load.start()

    barrier = pltpu.get_barrier_semaphore()

    def greet(rr, zz):
        pl.semaphore_signal(barrier, inc=1, device_id=(rr, zz), device_id_type=MESH)

    @pl.loop(1, NZ)
    def _(k):
        greet(r, lax.rem(z + k, NZ))

    @pl.loop(1, NS)
    def _(k):
        greet(lax.rem(r + k, NS), z)

    for i in range(2):
        for sp in range(2):
            rr = i * 16 + 2 * z + sp

            @pl.when(rr != r)
            def _():
                @pl.loop(1, NZ)
                def _(k):
                    greet(rr, lax.rem(z + k, NZ))

    def remote(src, dst, phase, rr, zz):
        return pltpu.make_async_remote_copy(
            src_ref=src,
            dst_ref=dst,
            send_sem=send_sem.at[phase],
            recv_sem=recv_sem.at[phase],
            device_id=(rr, zz),
            device_id_type=MESH,
        )

    def arrived(ref, phase):
        pltpu.make_async_copy(ref, ref, recv_sem.at[phase]).wait()

    def sent(ref, phase):
        pltpu.make_async_copy(ref, ref, send_sem.at[phase]).wait()

    loads[0].wait()
    loads[1].wait()
    phi = phv[...]
    for i in range(2):
        part = nt(phi, pv[i])
        for b in range(4):
            asend[i * 4 + b] = part[:, b * LANE : (b + 1) * LANE]

    extra = jnp.where(owner == z, 0, NS - 1)
    pl.semaphore_wait(barrier, NZ - 1 + NS - 1 + extra)

    @pl.loop(1, NZ)
    def _(k):
        zz = lax.rem(z + k, NZ)
        remote(asend.at[zz], arecv.at[z], 0, r, zz).start()

    arecv[z] = asend[z]
    arrived(arecv.at[pl.ds(0, NZ - 1)], 0)
    total = arecv[0]
    for k in range(1, NZ):
        total = total + arecv[k]
    logit[z] = total

    @pl.loop(1, NZ)
    def _(k):
        zz = lax.rem(z + k, NZ)
        remote(logit.at[z], logit.at[z], 1, r, zz).start()

    arrived(logit.at[pl.ds(0, NZ - 1)], 1)
    loads[2].wait()

    diag = iota((32, LANE), 0) == iota((32, LANE), 1)
    peaks, sums = [], []
    for i in range(2):
        li = jnp.concatenate([logit[i * 4 + b] for b in range(4)], axis=1)
        peak = jnp.max(li, axis=1, keepdims=True)
        e = jnp.exp(li - peak)
        peaks.append(peak)
        sums.append(jnp.sum(e, axis=1, keepdims=True))
        hi = e.astype(BF16)
        lo = (e - hi.astype(F32)).astype(BF16)
        both = nn(jnp.concatenate([hi, lo], axis=0), pv[i])
        slot_part = both[:16] + both[16:]
        ec = jnp.exp(li - jnp.max(li, axis=0, keepdims=True))
        combine_b = (ec / jnp.sum(ec, axis=0, keepdims=True)).astype(BF16)
        grad_part = nn(combine_b, gv[i])
        for half in range(2):
            for c in range(4):
                base = (i * 16 + half * 8) * 16 + c
                rows = slice(half * 8, half * 8 + 8)
                lanes = slice(c * LANE, (c + 1) * LANE)
                csend[pl.ds(base, 8, stride=16), :] = slot_part[rows, lanes]
                csend[pl.ds(base + 4, 8, stride=16), :] = grad_part[rows, lanes]
    peak_col = jnp.concatenate(peaks, axis=0)
    sum_col = jnp.concatenate(sums, axis=0)
    peak_row = jnp.sum(jnp.where(diag, peak_col, 0.0), axis=0, keepdims=True)
    sum_row = jnp.sum(jnp.where(diag, sum_col, 0.0), axis=0, keepdims=True)
    csend[pl.ds(8, 32, stride=16), :] = jnp.broadcast_to(peak_row, (32, LANE))
    csend[pl.ds(9, 32, stride=16), :] = jnp.broadcast_to(sum_row, (32, LANE))

    mine = pl.ds(pl.multiple_of(r * 16, 16), 16)

    @pl.loop(1, NS)
    def _(k):
        rr = lax.rem(r + k, NS)
        there = pl.ds(pl.multiple_of(rr * 16, 16), 16)
        remote(csend.at[there], crecv.at[mine], 2, rr, z).start()

    crecv[mine, :] = csend[mine, :]
    arrived(crecv.at[pl.ds(0, 16 * (NS - 1))], 2)

    peak_all = crecv[pl.ds(8, 32, stride=16), :]
    sum_all = crecv[pl.ds(9, 32, stride=16), :]
    top = jnp.max(peak_all, axis=0, keepdims=True)
    scale = jnp.exp(peak_all - top)
    denom = jnp.sum(scale * sum_all, axis=0, keepdims=True)
    lse_row = top + jnp.log(denom)
    lse_col = jnp.sum(jnp.where(diag, lse_row, 0.0), axis=1, keepdims=True)
    lse_b[...] = jnp.broadcast_to(lse_col, (32, LANE))
    weight = jnp.sum(
        jnp.where(iota((32, LANE), 1) == r, scale / denom, 0.0), axis=1, keepdims=True
    )
    dtmp[...] = jnp.zeros((16, LANE), F32)
    for c in range(4):
        row = jnp.sum(weight * crecv[pl.ds(c, 32, stride=16), :], axis=0, keepdims=True)
        high = row.astype(BF16).astype(F32)
        dtmp[c : c + 1, :] = high
        dtmp[4 + c : 5 + c, :] = row - high
        dtmp[8 + c : 9 + c, :] = jnp.sum(
            crecv[pl.ds(4 + c, 32, stride=16), :], axis=0, keepdims=True
        )
    dsend[...] = dtmp[...].astype(BF16)

    dplace = drecv.at[
        pl.ds(pl.multiple_of(q * 16, 16), 16), pl.ds(pl.multiple_of(z * LANE, LANE), LANE)
    ]

    @pl.when(owner != z)
    def _():
        remote(dsend, dplace, 3, r, owner).start()

    @pl.when(owner == z)
    def _():
        pltpu.make_async_copy(dsend, dplace, recv_sem.at[3]).start()

    @pl.loop(1, NS)
    def _(k):
        remote(dsend, dplace, 3, lax.rem(r + k, NS), owner).start()

    at = iota((96, 64), 0)
    c_of, j = at // 24, lax.rem(at, 24)
    part_of = jnp.where(j < 8, 0, jnp.where(j < 16, 8, 4))
    want = lax.rem(j, 4) * 16 + part_of + c_of
    pick = jnp.where(iota((96, 64), 1) == want, 1.0, 0.0).astype(BF16)

    arrived(drecv, 3)
    picked = nn(pick, drecv[...])
    for c in range(4):
        for b in range(NZ):
            rows_f[:, (b * 4 + c) * LANE : (b * 4 + c + 1) * LANE] = picked[
                c * 24 : c * 24 + 24, b * LANE : (b + 1) * LANE
            ]
    loads[3].wait()
    loads[4].wait()
    lhs = rows_f[0:16, :].astype(BF16)
    hidden = nn(lhs, wiv[0])[0:8]
    act_grad = nt(lhs, wov[0])[8:16]
    inner = slope_coef * (hidden + cubic_coef * hidden * hidden * hidden)
    tangent = jnp.tanh(inner)
    active = 0.5 * hidden * (1.0 + tangent)
    slope = 0.5 * (1.0 + tangent) + 0.5 * hidden * (1.0 - tangent * tangent) * slope_coef * (
        1.0 + 3.0 * cubic_coef * hidden * hidden
    )
    pre = act_grad * slope
    upper = iota((8, 256), 0) < 4
    none = jnp.zeros((8, 256), F32)
    active = jnp.where(upper, active, 0.0)
    pre = jnp.where(upper, 0.0, pre)
    active_lo = jnp.concatenate([active, none], axis=0).astype(BF16)
    active_hi = jnp.concatenate([none, active], axis=0).astype(BF16)
    pre_lo = jnp.concatenate([pre, none], axis=0).astype(BF16)
    esend[...] = (nn(active_lo, wov[0]) + nt(pre_lo, wiv[0]))[0:8]

    own = pl.ds(pl.multiple_of(tile_of(r) * LANE, LANE), LANE)

    @pl.loop(1, NS)
    def _(k):
        rr = lax.rem(r + k, NS)
        lanes = pl.ds(pl.multiple_of(tile_of(rr) * LANE, LANE), LANE)
        remote(esend.at[:, lanes], erecv.at[r], 4, rr, z).start()

    erecv[r] = esend[:, own]

    gwov[0] = tn(active_hi, lhs).astype(BF16)
    gwiv[0] = tn(lhs, pre_lo).astype(BF16)
    stores = [
        pltpu.make_async_copy(gwiv, grad_w_in, out_sem.at[0]),
        pltpu.make_async_copy(gwov, grad_w_out, out_sem.at[1]),
    ]
    for store in stores:
        store.start()

    arrived(erecv.at[pl.ds(0, NS - 1)], 4)
    total = erecv[0]
    for k in range(1, NS):
        total = total + erecv[k]
    total = total.astype(BF16).astype(F32)
    slot_in = rows_f[0:8, own] + rows_f[16:24, own]
    product = total * slot_in
    high = product.astype(BF16).astype(F32)
    rest = pltpu.roll(product - high, 4, 0)
    fsend[...] = jnp.concatenate(
        [total, jnp.where(iota((8, LANE), 0) < 4, rest, high)], axis=0
    ).astype(BF16)

    fplace = frecv.at[
        pl.ds(pl.multiple_of(z * 16, 16), 16), pl.ds(pl.multiple_of(q * LANE, LANE), LANE)
    ]

    @pl.when(owner != z)
    def _():
        remote(fsend, fplace, 5, r, owner).start()

    @pl.when(owner == z)
    def _():
        pltpu.make_async_copy(fsend, fplace, recv_sem.at[5]).start()

    @pl.loop(1, NS)
    def _(k):
        remote(fsend, fplace, 5, lax.rem(r + k, NS), owner).start()

    at = iota((96, LANE), 0)
    kind, slot = at // 32, lax.rem(at, 16)
    want = (slot // 2) * 16 + kind * 4 + (lax.rem(at, 32) // 16) * 2 + lax.rem(slot, 2)
    col = iota((96, LANE), 1)
    pick = jnp.where(
        (col == want) | ((kind == 2) & (col == want + 4)), 1.0, 0.0
    ).astype(BF16)

    arrived(frecv, 5)
    picked = nn(pick, frecv[...])
    slot_out = picked[0:32].astype(BF16)
    input_grad = picked[32:64].astype(BF16)
    col_part = jnp.sum(picked[64:96], axis=1, keepdims=True)
    for i in range(2):
        rows = slice(i * 16, i * 16 + 16)
        comb_part = nt(slot_out[rows], gv[i])
        disp_part = nt(input_grad[rows], pv[i]) - col_part[rows]
        for b in range(4):
            lanes = slice(b * LANE, (b + 1) * LANE)
            gsend[i * 4 + b, 0:16] = comb_part[:, lanes]
            gsend[i * 4 + b, 16:32] = disp_part[:, lanes]

    @pl.loop(1, NZ)
    def _(k):
        zz = lax.rem(z + k, NZ)
        remote(gsend.at[zz], grecv.at[z], 6, r, zz).start()

    grecv[z] = gsend[z]
    chunk = logit[z]
    ec = jnp.exp(chunk - jnp.max(chunk, axis=0, keepdims=True))
    combine = ec / jnp.sum(ec, axis=0, keepdims=True)
    dispatch = jnp.exp(chunk - lse_b[pl.ds(pl.multiple_of((z // 4) * 16, 16), 16), :])
    arrived(grecv.at[pl.ds(0, NZ - 1)], 6)
    total = grecv[0]
    for k in range(1, NZ):
        total = total + grecv[k]
    comb_grad, disp_grad = total[0:16], total[16:32]
    row_dots = jnp.sum(combine * comb_grad, axis=0, keepdims=True)
    hbuf[z] = (combine * (comb_grad - row_dots) + dispatch * disp_grad).astype(BF16)

    @pl.loop(1, NZ)
    def _(k):
        zz = lax.rem(z + k, NZ)
        remote(hbuf.at[z], hbuf.at[z], 7, r, zz).start()

    dispatch_b = []
    for i in range(2):
        li = jnp.concatenate([logit[i * 4 + b] for b in range(4)], axis=1)
        dispatch_b.append(jnp.exp(li - lse_col[i * 16 : i * 16 + 16]).astype(BF16))
    arrived(hbuf.at[pl.ds(0, NZ - 1)], 7)
    logit_b = [
        jnp.concatenate([hbuf[i * 4 + b] for b in range(4)], axis=1) for i in range(2)
    ]
    phi_part = nn(logit_b[0], pv[0]) + nn(logit_b[1], pv[1])
    for u in range(8):
        half, c = u // 4, u % 4
        isend[u] = phi_part[half * 8 : half * 8 + 8, c * LANE : (c + 1) * LANE]

    @pl.loop(0, 8)
    def _(u):
        @pl.when(4 * u != r)
        def _():
            remote(isend.at[u], irecv.at[r], 8, 4 * u, z).start()

    for i in range(2):
        left = jnp.concatenate([dispatch_b[i], logit_b[i]], axis=0)
        right = jnp.concatenate([input_grad[i * 16 : i * 16 + 16], phi], axis=0)
        gpv[i] = tn(left, right).astype(BF16)
    stores.append(pltpu.make_async_copy(gpv, grad_patches, out_sem.at[2]))
    stores[2].start()

    tile = r // 4

    @pl.when(lax.rem(r, 4) == 0)
    def _():
        irecv[r] = isend[tile]
        arrived(irecv.at[pl.ds(0, NS - 1)], 8)
        total = irecv[0]
        for k in range(1, NS):
            total = total + irecv[k]
        jbuf[tile] = total * (1.0 / math.sqrt(2 * 512 * NS))

        @pl.loop(1, NS)
        def _(k):
            remote(jbuf.at[tile], jbuf.at[tile], 9, lax.rem(r + k, NS), z).start()

        arrived(jbuf.at[pl.ds(0, 7)], 9)
        sent(irecv.at[pl.ds(0, NS - 1)], 9)
        sent(isend.at[pl.ds(0, 7)], 8)

    @pl.when(lax.rem(r, 4) != 0)
    def _():
        arrived(jbuf, 9)
        sent(isend, 8)

    for u in range(8):
        half, c = u // 4, u % 4
        gphv[half * 8 : half * 8 + 8, c * LANE : (c + 1) * LANE] = jbuf[u]
    stores.append(pltpu.make_async_copy(gphv, grad_phi, out_sem.at[3]))
    stores[3].start()

    sent(asend.at[pl.ds(0, NZ - 1)], 0)
    sent(logit.at[pl.ds(0, NZ - 1)], 1)
    sent(csend.at[pl.ds(0, 16 * (NS - 1))], 2)
    sent(esend.at[:, pl.ds(0, LANE * (NS - 1))], 4)
    sent(gsend.at[pl.ds(0, NZ - 1)], 6)
    sent(hbuf.at[pl.ds(0, NZ - 1)], 7)

    @pl.when(owner == z)
    def _():
        sent(drecv.at[:, pl.ds(0, 7 * LANE)], 3)
        sent(drecv.at[pl.ds(0, 48), pl.ds(0, LANE)], 3)
        sent(frecv.at[:, pl.ds(0, 3 * LANE)], 5)
        sent(frecv.at[pl.ds(0, 112), pl.ds(0, LANE)], 5)

    @pl.when(owner != z)
    def _():
        sent(drecv, 3)
        sent(frecv, 5)

    for store in stores:
        store.wait()


def local(patches, grad_out, phi_t, w_in, w_out):
    anywhere = pl.BlockSpec(memory_space=pl.ANY)
    vmem = pltpu.VMEM
    return pl.pallas_call(
        kernel,
        out_shape=(
            jax.ShapeDtypeStruct(patches.shape, BF16),
            jax.ShapeDtypeStruct(phi_t.shape, F32),
            jax.ShapeDtypeStruct(w_in.shape, BF16),
            jax.ShapeDtypeStruct(w_out.shape, BF16),
        ),
        in_specs=[anywhere] * 5,
        out_specs=[anywhere] * 4,
        scratch_shapes=[
            vmem((2, 512, 512), BF16),
            vmem((2, 512, 512), BF16),
            vmem((16, 512), BF16),
            vmem((1, 4096, 256), BF16),
            vmem((1, 256, 4096), BF16),
            vmem((2, 512, 512), BF16),
            vmem((16, 512), F32),
            vmem((1, 4096, 256), BF16),
            vmem((1, 256, 4096), BF16),
            vmem((8, 16, LANE), F32),
            vmem((8, 16, LANE), F32),
            vmem((8, 16, LANE), F32),
            vmem((512, LANE), F32),
            vmem((512, LANE), F32),
            vmem((16, LANE), F32),
            vmem((16, LANE), BF16),
            vmem((64, 1024), BF16),
            vmem((24, 4096), F32),
            vmem((8, 4096), F32),
            vmem((32, 8, LANE), F32),
            vmem((16, LANE), BF16),
            vmem((LANE, 512), BF16),
            vmem((32, LANE), F32),
            vmem((8, 32, LANE), F32),
            vmem((8, 32, LANE), F32),
            vmem((8, 16, LANE), BF16),
            vmem((8, 8, LANE), F32),
            vmem((32, 8, LANE), F32),
            vmem((8, 8, LANE), F32),
            pltpu.SemaphoreType.DMA((5,)),
            pltpu.SemaphoreType.DMA((4,)),
            pltpu.SemaphoreType.DMA((10,)),
            pltpu.SemaphoreType.DMA((10,)),
        ],
        compiler_params=pltpu.CompilerParams(
            collective_id=0, has_side_effects=True, vmem_limit_bytes=48 * 1024 * 1024
        ),
        cost_estimate=pl.CostEstimate(
            flops=400_000_000, bytes_accessed=12_000_000, transcendentals=100_000
        ),
    )(patches, grad_out, phi_t, w_in, w_out)


def solution(mesh):
    in_specs = (
        P(None, "seq", "exp"),
        P(None, "seq", "exp"),
        P(None, "exp"),
        P("exp", None, "seq"),
        P("exp", "seq", None),
    )
    out_specs = (
        P(None, "seq", "exp"),
        P(None, "exp"),
        P("exp", None, "seq"),
        P("exp", "seq", None),
    )
    return jax.shard_map(local, mesh=mesh, in_specs=in_specs, out_specs=out_specs, check_vma=False)
```

time: 913 us -> 97.4 us (0.11)
  blocking collectives: 672 us -> 0 us
  waiting for transfers between devices: 156 us -> 0 us
  Pallas kernels: 0 us -> 88.1 us
  matrix products: 30.9 us -> 0 us
  local copies, waits for them, and re-layouts: 23.7 us -> 8.41 us
  between operations: 14.2 us -> 0.65 us
  starting transfers between devices: 10.9 us -> 0 us
    psum x5 -> x0, blocking collectives: 567 us -> none  [the longest x1 131 us: local(): slot_outputs = lax.psum(out_part, 'seq').astype(jnp.bfloat16)]
    pallas_call x0 -> x1, Pallas kernels: none -> 88.1 us  [local(): pl.pallas_call(kernel, out_shape=(jax.ShapeDtypeStruct(patches.shape, BF1...]
    all_gather x1 -> x0, waiting for transfers between devices: 76.5 us -> none  [local(): lax.all_gather(patches, 'exp', axis=2, tiled=True)]
    psum x1 -> x0, waiting for transfers between devices: 64.1 us -> none  [local(): comb_grad = lax.psum(comb_part, 'exp')]
    pmax x1 -> x0, blocking collectives: 62.7 us -> none  [local(): col_peak = lax.pmax(jnp.max(logits, axis=1), 'seq')]
    all_gather x2 -> x0, blocking collectives: 42.5 us -> none  [the longest x1 23.8 us: local(): lax.all_gather(phi_t, 'exp', axis=1, tiled=True)]
    dot_general x14 -> x0, matrix products: 30.9 us -> none  [the longest x1 6.84 us: local(): jnp.einsum('ipd,isd->ips', full_rows, all_grads, preferred_element_type=j...]
    all_to_all x3 -> x0, waiting for transfers between devices: 14.8 us -> none  [the longest x1 6.75 us: local(): lax.all_to_all(slot_grads, 'exp', split_axis=1, concat_axis=2, tiled=True)]
  transfers between devices with their start and end apart: 5 -> 0, of which waited for: 5 -> 0; matrix products, arithmetic and copies ran while one was open for 1% -> 0% of each run, Pallas kernels for 0% -> 0%
where the time goes in v1:
time: 97.4 us; the launch traced here: 97.2 us
  Pallas kernels  88.1 us (90%)
  local copies, waits for them, and re-layouts  8.41 us (9%)
    pallas_call x1, Pallas kernels, local(): pl.pallas_call(kernel, out_shape=(jax.ShapeDtypeStruct(patches.shape, BF1...  88.1 us
    unnamed x12, local copies, waits for them, and re-layouts  8.41 us

profile of v1, /device:TPU:1, one launch (start us, length us, event | category | flops | bytes accessed | tf_op | source)
XLA Modules:
  0.0 97.2 jit_solution(1386020515328167115)
XLA Ops:
  0.6 0.0 copy-start
  0.6 1.2 %copy-done = bf16[2,512,512]{2,1,0:T(8,128)(2,1)S(1)} copy-done((bf16[2,512,512]{2,1,0:T(8,128)(2,1)S(1)}, bf16[2,512,512]{2,1,0:T(8,128)(2,1)}, u32[]{:S(2)}) %copy-start) | copy-done | bytes 1048600
  1.9 0.0 copy-start.1
  1.9 1.2 %copy-done.1 = bf16[2,512,512]{2,1,0:T(8,128)(2,1)S(1)} copy-done((bf16[2,512,512]{2,1,0:T(8,128)(2,1)S(1)}, bf16[2,512,512]{2,1,0:T(8,128)(2,1)}, u32[]{:S(2)}) %copy-start.1) | copy-done | bytes 1048600
  3.1 0.0 copy-start.2
  3.1 0.7 copy-done.2
  3.8 88.1 %shard_map.84 = (bf16[2,512,512]{2,1,0:T(8,128)(2,1)S(1)}, f32[16,512]{1,0:T(8,128)S(1)}, bf16[1,4096,256]{2,1,0:T(8,128)(2,1)S(1)}, bf16[1,256,4096]{2,1,0:T(8,128)(2,1)}) custom-call(bf16[2,512,512]{2,1,0:T(8,128)(2,1)S(1)} %copy-done, bf16[2,512,512]{2,1,0:T(8,128)(2,1)S(1)} %copy-done.1, bf16[16,512]{1,0:T(8,128)(2,1)S(1)} %copy-done.2, ...), custom_call_target="tpu_custom_call" | custom-call | flops 400000000 | bytes 12000000 | tf_op jit(solution)/shard_map/pallas_call | solution.py:420
  91.9 1.0 %copy.13 = bf16[2,512,512]{2,1,0:T(8,128)(2,1)} copy(bf16[2,512,512]{2,1,0:T(8,128)(2,1)S(1)} %get-tuple-element.8) | data formatting | bytes 2097152
  92.9 0.6 copy.14
  93.5 0.0 copy-start.3
  93.5 1.3 %copy.15 = bf16[1,4096,256]{2,1,0:T(8,128)(2,1)} copy(bf16[1,4096,256]{2,1,0:T(8,128)(2,1)S(1)} %get-tuple-element.10) | data formatting | bytes 4194304
  94.8 1.0 %copy-done.3 = bf16[1,256,4096]{2,1,0:T(8,128)(2,1)S(1)} copy-done((bf16[1,256,4096]{2,1,0:T(8,128)(2,1)S(1)}, bf16[1,256,4096]{2,1,0:T(8,128)(2,1)}, u32[]{:S(2)}) %copy-start.3) | copy-done | bytes 2097176
  95.9 1.3 %copy.16 = bf16[1,256,4096]{2,1,0:T(8,128)(2,1)} copy(bf16[1,256,4096]{2,1,0:T(8,128)(2,1)S(1)} %copy-done.3) | data formatting | bytes 4194304
Async XLA Ops:
  0.6 1.2 %copy-start = (bf16[2,512,512]{2,1,0:T(8,128)(2,1)S(1)}, bf16[2,512,512]{2,1,0:T(8,128)(2,1)}, u32[]{:S(2)}) copy-start(bf16[2,512,512]{2,1,0:T(8,128)(2,1)} %patches.1) | copy-start | bytes 3145732
  1.9 1.2 %copy-start.1 = (bf16[2,512,512]{2,1,0:T(8,128)(2,1)S(1)}, bf16[2,512,512]{2,1,0:T(8,128)(2,1)}, u32[]{:S(2)}) copy-start(bf16[2,512,512]{2,1,0:T(8,128)(2,1)} %grad_out.1) | copy-start | bytes 3145732
  3.1 0.7 copy-start.2
  93.5 2.3 %copy-start.3 = (bf16[1,256,4096]{2,1,0:T(8,128)(2,1)S(1)}, bf16[1,256,4096]{2,1,0:T(8,128)(2,1)}, u32[]{:S(2)}) copy-start(bf16[1,256,4096]{2,1,0:T(8,128)(2,1)} %get-tuple-element.11) | copy-start | bytes 6291460

commit v2 on v1

--- a/solution.py
+++ b/solution.py
@@ -35,21 +35,31 @@
     return lax.broadcasted_iota(jnp.int32, shape, dim)
 
 
+def thirds(value):
+    first = value.astype(BF16).astype(F32)
+    second = (value - first).astype(BF16).astype(F32)
+    return first, second, value - first - second
+
+
+def spread(column):
+    first, second, third = thirds(column)
+    lane = iota((8, LANE), 1)
+    return jnp.where(
+        lane == 0, first, jnp.where(lane == 1, second, jnp.where(lane == 2, third, 0.0))
+    )
+
+
 def kernel(
     patches, grad_out, phi_t, w_in, w_out,
     grad_patches, grad_phi, grad_w_in, grad_w_out,
     pv, gv, phv, wiv, wov, gpv, gphv, gwiv, gwov,
-    asend, arecv, logit, csend, crecv, dtmp, dsend, drecv, rows_f,
-    esend, erecv, fsend, frecv, lse_b, gsend, grecv, hbuf, isend, irecv, jbuf,
+    asend, arecv, logit, cfull, csend, crecv, dtmp, dsend, drecv, rows_f,
+    esend, erecv, fsend, frecv, lse_b, dots_b, gsend, grecv, hbuf, isend, irecv, jbuf,
     in_sem, out_sem, send_sem, recv_sem,
 ):
     r = lax.axis_index("seq")
     z = lax.axis_index("exp")
-    owner = lax.rem(r, 16) // 2
-    q = (r // 16) * 2 + lax.rem(r, 2)
-
-    def tile_of(rr):
-        return (lax.rem(rr, 16) // 2) * 4 + (rr // 16) * 2 + lax.rem(rr, 2)
+    source, q = r // 4, lax.rem(r, 4)
 
     loads = [
         pltpu.make_async_copy(src, dst, in_sem.at[k])
@@ -73,15 +83,11 @@
     def _(k):
         greet(lax.rem(r + k, NS), z)
 
-    for i in range(2):
-        for sp in range(2):
-            rr = i * 16 + 2 * z + sp
-
-            @pl.when(rr != r)
-            def _():
-                @pl.loop(1, NZ)
-                def _(k):
-                    greet(rr, lax.rem(z + k, NZ))
+    @pl.when(source != z)
+    def _():
+        @pl.loop(1, NS)
+        def _(k):
+            greet(lax.rem(r + k, NS), source)
 
     def remote(src, dst, phase, rr, zz):
         return pltpu.make_async_remote_copy(
@@ -96,8 +102,24 @@
     def arrived(ref, phase):
         pltpu.make_async_copy(ref, ref, recv_sem.at[phase]).wait()
 
+    dwait = fwait = csend.at[pl.ds(0, 16 * (NS - 1))]
+
     def sent(ref, phase):
         pltpu.make_async_copy(ref, ref, send_sem.at[phase]).wait()
+
+    def scatter(piece, place, phase):
+        @pl.loop(0, NS)
+        def _(k):
+            e, qq = lax.rem(z + 1 + k // 4, NZ), lax.rem(r + k, 4)
+            rr = z * 4 + qq
+
+            @pl.when((rr != r) | (e != z))
+            def _():
+                remote(piece(qq, e), place, phase, rr, e).start()
+
+            @pl.when((rr == r) & (e == z))
+            def _():
+                pltpu.make_async_copy(piece(qq, e), place, recv_sem.at[phase]).start()
 
     loads[0].wait()
     loads[1].wait()
@@ -107,7 +129,7 @@
         for b in range(4):
             asend[i * 4 + b] = part[:, b * LANE : (b + 1) * LANE]
 
-    extra = jnp.where(owner == z, 0, NS - 1)
+    extra = jnp.where(source == z, 3 * (NZ - 1), 4 * (NZ - 1))
     pl.semaphore_wait(barrier, NZ - 1 + NS - 1 + extra)
 
     @pl.loop(1, NZ)
@@ -134,7 +156,7 @@
     peaks, sums = [], []
     for i in range(2):
         li = jnp.concatenate([logit[i * 4 + b] for b in range(4)], axis=1)
-        peak = jnp.max(li, axis=1, keepdims=True)
+        peak = jnp.max(li, axis=1, keepdims=True).astype(BF16).astype(F32)
         e = jnp.exp(li - peak)
         peaks.append(peak)
         sums.append(jnp.sum(e, axis=1, keepdims=True))
@@ -150,63 +172,62 @@
                 base = (i * 16 + half * 8) * 16 + c
                 rows = slice(half * 8, half * 8 + 8)
                 lanes = slice(c * LANE, (c + 1) * LANE)
-                csend[pl.ds(base, 8, stride=16), :] = slot_part[rows, lanes]
-                csend[pl.ds(base + 4, 8, stride=16), :] = grad_part[rows, lanes]
+                high = slot_part[rows, lanes].astype(BF16).astype(F32)
+                cfull[pl.ds(base, 8, stride=16), :] = high
+                cfull[pl.ds(base + 4, 8, stride=16), :] = slot_part[rows, lanes] - high
+                cfull[pl.ds(base + 8, 8, stride=16), :] = grad_part[rows, lanes]
     peak_col = jnp.concatenate(peaks, axis=0)
     sum_col = jnp.concatenate(sums, axis=0)
     peak_row = jnp.sum(jnp.where(diag, peak_col, 0.0), axis=0, keepdims=True)
     sum_row = jnp.sum(jnp.where(diag, sum_col, 0.0), axis=0, keepdims=True)
-    csend[pl.ds(8, 32, stride=16), :] = jnp.broadcast_to(peak_row, (32, LANE))
-    csend[pl.ds(9, 32, stride=16), :] = jnp.broadcast_to(sum_row, (32, LANE))
-
-    mine = pl.ds(pl.multiple_of(r * 16, 16), 16)
-
-    @pl.loop(1, NS)
-    def _(k):
-        rr = lax.rem(r + k, NS)
-        there = pl.ds(pl.multiple_of(rr * 16, 16), 16)
-        remote(csend.at[there], crecv.at[mine], 2, rr, z).start()
-
-    crecv[mine, :] = csend[mine, :]
-    arrived(crecv.at[pl.ds(0, 16 * (NS - 1))], 2)
-
-    peak_all = crecv[pl.ds(8, 32, stride=16), :]
-    sum_all = crecv[pl.ds(9, 32, stride=16), :]
+    stats = (peak_row,) + thirds(sum_row)
+    for k, row in enumerate(stats):
+        cfull[pl.ds(12 + k, 32, stride=16), :] = jnp.broadcast_to(row, (32, LANE))
+    csend[...] = cfull[...].astype(BF16)
+
+    def piece(qq, e):
+        row = (qq // 2) * 16 + e * 2 + lax.rem(qq, 2)
+        return csend.at[pl.ds(pl.multiple_of(row * 16, 16), 16)]
+
+    scatter(piece, crecv.at[pl.ds(pl.multiple_of(r * 16, 16), 16)], 2)
+    arrived(crecv, 2)
+    cfull[...] = crecv[...].astype(F32)
+    peak_all = cfull[pl.ds(12, 32, stride=16), :]
+    sum_all = (
+        cfull[pl.ds(13, 32, stride=16), :]
+        + cfull[pl.ds(14, 32, stride=16), :]
+        + cfull[pl.ds(15, 32, stride=16), :]
+    )
     top = jnp.max(peak_all, axis=0, keepdims=True)
     scale = jnp.exp(peak_all - top)
     denom = jnp.sum(scale * sum_all, axis=0, keepdims=True)
     lse_row = top + jnp.log(denom)
     lse_col = jnp.sum(jnp.where(diag, lse_row, 0.0), axis=1, keepdims=True)
     lse_b[...] = jnp.broadcast_to(lse_col, (32, LANE))
+    mine = (q // 2) * 16 + z * 2 + lax.rem(q, 2)
     weight = jnp.sum(
-        jnp.where(iota((32, LANE), 1) == r, scale / denom, 0.0), axis=1, keepdims=True
+        jnp.where(iota((32, LANE), 1) == mine, scale / denom, 0.0), axis=1, keepdims=True
     )
     dtmp[...] = jnp.zeros((16, LANE), F32)
     for c in range(4):
-        row = jnp.sum(weight * crecv[pl.ds(c, 32, stride=16), :], axis=0, keepdims=True)
+        part = cfull[pl.ds(c, 32, stride=16), :] + cfull[pl.ds(4 + c, 32, stride=16), :]
+        row = jnp.sum(weight * part, axis=0, keepdims=True)
         high = row.astype(BF16).astype(F32)
         dtmp[c : c + 1, :] = high
         dtmp[4 + c : 5 + c, :] = row - high
         dtmp[8 + c : 9 + c, :] = jnp.sum(
-            crecv[pl.ds(4 + c, 32, stride=16), :], axis=0, keepdims=True
+            cfull[pl.ds(8 + c, 32, stride=16), :], axis=0, keepdims=True
         )
     dsend[...] = dtmp[...].astype(BF16)
 
-    dplace = drecv.at[
-        pl.ds(pl.multiple_of(q * 16, 16), 16), pl.ds(pl.multiple_of(z * LANE, LANE), LANE)
-    ]
-
-    @pl.when(owner != z)
-    def _():
-        remote(dsend, dplace, 3, r, owner).start()
-
-    @pl.when(owner == z)
-    def _():
-        pltpu.make_async_copy(dsend, dplace, recv_sem.at[3]).start()
+    drows = pl.ds(pl.multiple_of(q * 16, 16), 16)
+    dlanes = pl.ds(pl.multiple_of(source * LANE, LANE), LANE)
 
     @pl.loop(1, NS)
     def _(k):
-        remote(dsend, dplace, 3, lax.rem(r + k, NS), owner).start()
+        remote(dsend, drecv.at[drows, dlanes], 3, lax.rem(r + k, NS), z).start()
+
+    drecv[drows, dlanes] = dsend[...]
 
     at = iota((96, 64), 0)
     c_of, j = at // 24, lax.rem(at, 24)
@@ -214,7 +235,7 @@
     want = lax.rem(j, 4) * 16 + part_of + c_of
     pick = jnp.where(iota((96, 64), 1) == want, 1.0, 0.0).astype(BF16)
 
-    arrived(drecv, 3)
+    arrived(dwait, 3)
     picked = nn(pick, drecv[...])
     for c in range(4):
         for b in range(NZ):
@@ -240,17 +261,19 @@
     active_lo = jnp.concatenate([active, none], axis=0).astype(BF16)
     active_hi = jnp.concatenate([none, active], axis=0).astype(BF16)
     pre_lo = jnp.concatenate([pre, none], axis=0).astype(BF16)
-    esend[...] = (nn(active_lo, wov[0]) + nt(pre_lo, wiv[0]))[0:8]
-
-    own = pl.ds(pl.multiple_of(tile_of(r) * LANE, LANE), LANE)
-
-    @pl.loop(1, NS)
-    def _(k):
-        rr = lax.rem(r + k, NS)
-        lanes = pl.ds(pl.multiple_of(tile_of(rr) * LANE, LANE), LANE)
-        remote(esend.at[:, lanes], erecv.at[r], 4, rr, z).start()
-
-    erecv[r] = esend[:, own]
+    result = (nn(active_lo, wov[0]) + nt(pre_lo, wiv[0]))[0:8]
+    wide = iota((8, 4096), 0) < 4
+    dots = jnp.sum(result * (rows_f[0:8, :] + rows_f[16:24, :]), axis=1, keepdims=True)
+    high = result.astype(BF16).astype(F32)
+    rest = pltpu.roll(result - high, 4, 0)
+    esend[...] = jnp.concatenate(
+        [high, jnp.where(wide, rest, jnp.concatenate([spread(dots)] * 32, axis=1))], axis=0
+    ).astype(BF16)
+
+    def block(qq, e):
+        return esend.at[:, pl.ds(pl.multiple_of((e * 4 + qq) * LANE, LANE), LANE)]
+
+    scatter(block, erecv.at[r], 4)
 
     gwov[0] = tn(active_hi, lhs).astype(BF16)
     gwiv[0] = tn(lhs, pre_lo).astype(BF16)
@@ -261,52 +284,41 @@
     for store in stores:
         store.start()
 
-    arrived(erecv.at[pl.ds(0, NS - 1)], 4)
-    total = erecv[0]
+    arrived(erecv, 4)
+    total = erecv[0].astype(F32)
     for k in range(1, NS):
-        total = total + erecv[k]
-    total = total.astype(BF16).astype(F32)
-    slot_in = rows_f[0:8, own] + rows_f[16:24, own]
-    product = total * slot_in
-    high = product.astype(BF16).astype(F32)
-    rest = pltpu.roll(product - high, 4, 0)
+        total = total + erecv[k].astype(F32)
+    lower = iota((8, LANE), 0) < 4
+    rest = pltpu.roll(total[8:16], 4, 0)
+    dots = spread(jnp.sum(rest, axis=1, keepdims=True))
     fsend[...] = jnp.concatenate(
-        [total, jnp.where(iota((8, LANE), 0) < 4, rest, high)], axis=0
+        [jnp.where(lower, total[0:8], total[0:8] + rest), jnp.where(lower, dots, 0.0)], axis=0
     ).astype(BF16)
 
-    fplace = frecv.at[
-        pl.ds(pl.multiple_of(z * 16, 16), 16), pl.ds(pl.multiple_of(q * LANE, LANE), LANE)
-    ]
-
-    @pl.when(owner != z)
-    def _():
-        remote(fsend, fplace, 5, r, owner).start()
-
-    @pl.when(owner == z)
-    def _():
-        pltpu.make_async_copy(fsend, fplace, recv_sem.at[5]).start()
+    frows = pl.ds(pl.multiple_of(source * 16, 16), 16)
+    flanes = pl.ds(pl.multiple_of(q * LANE, LANE), LANE)
 
     @pl.loop(1, NS)
     def _(k):
-        remote(fsend, fplace, 5, lax.rem(r + k, NS), owner).start()
+        remote(fsend, frecv.at[frows, flanes], 5, lax.rem(r + k, NS), z).start()
+
+    frecv[frows, flanes] = fsend[...]
 
     at = iota((96, LANE), 0)
     kind, slot = at // 32, lax.rem(at, 16)
     want = (slot // 2) * 16 + kind * 4 + (lax.rem(at, 32) // 16) * 2 + lax.rem(slot, 2)
     col = iota((96, LANE), 1)
-    pick = jnp.where(
-        (col == want) | ((kind == 2) & (col == want + 4)), 1.0, 0.0
-    ).astype(BF16)
-
-    arrived(frecv, 5)
+    pick = jnp.where(col == want, 1.0, 0.0).astype(BF16)
+
+    arrived(fwait, 5)
     picked = nn(pick, frecv[...])
     slot_out = picked[0:32].astype(BF16)
     input_grad = picked[32:64].astype(BF16)
-    col_part = jnp.sum(picked[64:96], axis=1, keepdims=True)
+    dots_b[...] = jnp.broadcast_to(jnp.sum(picked[64:96, 0:LANE], axis=1, keepdims=True), (32, LANE))
     for i in range(2):
         rows = slice(i * 16, i * 16 + 16)
         comb_part = nt(slot_out[rows], gv[i])
-        disp_part = nt(input_grad[rows], pv[i]) - col_part[rows]
+        disp_part = nt(input_grad[rows], pv[i])
         for b in range(4):
             lanes = slice(b * LANE, (b + 1) * LANE)
             gsend[i * 4 + b, 0:16] = comb_part[:, lanes]
@@ -321,14 +333,16 @@
     chunk = logit[z]
     ec = jnp.exp(chunk - jnp.max(chunk, axis=0, keepdims=True))
     combine = ec / jnp.sum(ec, axis=0, keepdims=True)
-    dispatch = jnp.exp(chunk - lse_b[pl.ds(pl.multiple_of((z // 4) * 16, 16), 16), :])
+    image = pl.ds(pl.multiple_of((z // 4) * 16, 16), 16)
+    dispatch = jnp.exp(chunk - lse_b[image, :])
+    col_dots = dots_b[image, :]
     arrived(grecv.at[pl.ds(0, NZ - 1)], 6)
     total = grecv[0]
     for k in range(1, NZ):
         total = total + grecv[k]
     comb_grad, disp_grad = total[0:16], total[16:32]
     row_dots = jnp.sum(combine * comb_grad, axis=0, keepdims=True)
-    hbuf[z] = (combine * (comb_grad - row_dots) + dispatch * disp_grad).astype(BF16)
+    hbuf[z] = (combine * (comb_grad - row_dots) + dispatch * (disp_grad - col_dots)).astype(BF16)
 
     @pl.loop(1, NZ)
     def _(k):
@@ -393,22 +407,20 @@
 
     sent(asend.at[pl.ds(0, NZ - 1)], 0)
     sent(logit.at[pl.ds(0, NZ - 1)], 1)
-    sent(csend.at[pl.ds(0, 16 * (NS - 1))], 2)
-    sent(esend.at[:, pl.ds(0, LANE * (NS - 1))], 4)
+    sent(dwait, 3)
+    sent(fwait, 5)
     sent(gsend.at[pl.ds(0, NZ - 1)], 6)
     sent(hbuf.at[pl.ds(0, NZ - 1)], 7)
 
-    @pl.when(owner == z)
+    @pl.when(source == z)
     def _():
-        sent(drecv.at[:, pl.ds(0, 7 * LANE)], 3)
-        sent(drecv.at[pl.ds(0, 48), pl.ds(0, LANE)], 3)
-        sent(frecv.at[:, pl.ds(0, 3 * LANE)], 5)
-        sent(frecv.at[pl.ds(0, 112), pl.ds(0, LANE)], 5)
-
-    @pl.when(owner != z)
+        sent(crecv.at[pl.ds(0, 16 * (NS - 1))], 2)
+        sent(erecv.at[pl.ds(0, NS - 1)], 4)
+
+    @pl.when(source != z)
     def _():
-        sent(drecv, 3)
-        sent(frecv, 5)
+        sent(crecv, 2)
+        sent(erecv, 4)
 
     for store in stores:
         store.wait()
@@ -441,15 +453,17 @@
             vmem((8, 16, LANE), F32),
             vmem((8, 16, LANE), F32),
             vmem((512, LANE), F32),
-            vmem((512, LANE), F32),
+            vmem((512, LANE), BF16),
+            vmem((512, LANE), BF16),
             vmem((16, LANE), F32),
             vmem((16, LANE), BF16),
             vmem((64, 1024), BF16),
             vmem((24, 4096), F32),
-            vmem((8, 4096), F32),
-            vmem((32, 8, LANE), F32),
+            vmem((16, 4096), BF16),
+            vmem((32, 16, LANE), BF16),
             vmem((16, LANE), BF16),
             vmem((LANE, 512), BF16),
+            vmem((32, LANE), F32),
             vmem((32, LANE), F32),
             vmem((8, 32, LANE), F32),
             vmem((8, 32, LANE), F32),

time: 97.4 us -> 84.8 us (0.87)
  Pallas kernels: 88.1 us -> 75.4 us
    pallas_call x1, Pallas kernels: 88.1 us -> 75.4 us  [local(): pl.pallas_call(kernel, out_shape=(jax.ShapeDtypeStruct(patches.shape, BF1...]
where the time goes in v2:
time: 84.8 us; the launch traced here: 84.5 us
  Pallas kernels  75.4 us (89%)
  local copies, waits for them, and re-layouts  8.41 us (10%)
    pallas_call x1, Pallas kernels, local(): pl.pallas_call(kernel, out_shape=(jax.ShapeDtypeStruct(patches.shape, BF1...  75.4 us
    unnamed x12, local copies, waits for them, and re-layouts  8.41 us

profile of v2, /device:TPU:1, one launch (start us, length us, event | category | flops | bytes accessed | tf_op | source)
XLA Modules:
  0.0 84.5 jit_solution(16021190512020349427)
XLA Ops:
  0.6 0.0 copy-start
  0.6 1.2 %copy-done = bf16[2,512,512]{2,1,0:T(8,128)(2,1)S(1)} copy-done((bf16[2,512,512]{2,1,0:T(8,128)(2,1)S(1)}, bf16[2,512,512]{2,1,0:T(8,128)(2,1)}, u32[]{:S(2)}) %copy-start) | copy-done | bytes 1048600
  1.9 0.0 copy-start.1
  1.9 1.2 %copy-done.1 = bf16[2,512,512]{2,1,0:T(8,128)(2,1)S(1)} copy-done((bf16[2,512,512]{2,1,0:T(8,128)(2,1)S(1)}, bf16[2,512,512]{2,1,0:T(8,128)(2,1)}, u32[]{:S(2)}) %copy-start.1) | copy-done | bytes 1048600
  3.1 0.0 copy-start.2
  3.1 0.7 copy-done.2
  3.8 75.4 %shard_map.84 = (bf16[2,512,512]{2,1,0:T(8,128)(2,1)S(1)}, f32[16,512]{1,0:T(8,128)S(1)}, bf16[1,4096,256]{2,1,0:T(8,128)(2,1)S(1)}, bf16[1,256,4096]{2,1,0:T(8,128)(2,1)}) custom-call(bf16[2,512,512]{2,1,0:T(8,128)(2,1)S(1)} %copy-done, bf16[2,512,512]{2,1,0:T(8,128)(2,1)S(1)} %copy-done.1, bf16[16,512]{1,0:T(8,128)(2,1)S(1)} %copy-done.2, ...), custom_call_target="tpu_custom_call" | custom-call | flops 400000000 | bytes 12000000 | tf_op jit(solution)/shard_map/pallas_call | solution.py:432
  79.3 1.0 %copy.13 = bf16[2,512,512]{2,1,0:T(8,128)(2,1)} copy(bf16[2,512,512]{2,1,0:T(8,128)(2,1)S(1)} %get-tuple-element.8) | data formatting | bytes 2097152
  80.2 0.6 copy.14
  80.8 0.0 copy-start.3
  80.8 1.3 %copy.15 = bf16[1,4096,256]{2,1,0:T(8,128)(2,1)} copy(bf16[1,4096,256]{2,1,0:T(8,128)(2,1)S(1)} %get-tuple-element.10) | data formatting | bytes 4194304
  82.2 1.0 %copy-done.3 = bf16[1,256,4096]{2,1,0:T(8,128)(2,1)S(1)} copy-done((bf16[1,256,4096]{2,1,0:T(8,128)(2,1)S(1)}, bf16[1,256,4096]{2,1,0:T(8,128)(2,1)}, u32[]{:S(2)}) %copy-start.3) | copy-done | bytes 2097176
  83.2 1.3 %copy.16 = bf16[1,256,4096]{2,1,0:T(8,128)(2,1)} copy(bf16[1,256,4096]{2,1,0:T(8,128)(2,1)S(1)} %copy-done.3) | data formatting | bytes 4194304
Async XLA Ops:
  0.6 1.2 %copy-start = (bf16[2,512,512]{2,1,0:T(8,128)(2,1)S(1)}, bf16[2,512,512]{2,1,0:T(8,128)(2,1)}, u32[]{:S(2)}) copy-start(bf16[2,512,512]{2,1,0:T(8,128)(2,1)} %patches.1) | copy-start | bytes 3145732
  1.9 1.2 %copy-start.1 = (bf16[2,512,512]{2,1,0:T(8,128)(2,1)S(1)}, bf16[2,512,512]{2,1,0:T(8,128)(2,1)}, u32[]{:S(2)}) copy-start(bf16[2,512,512]{2,1,0:T(8,128)(2,1)} %grad_out.1) | copy-start | bytes 3145732
  3.1 0.7 copy-start.2
  80.8 2.3 %copy-start.3 = (bf16[1,256,4096]{2,1,0:T(8,128)(2,1)S(1)}, bf16[1,256,4096]{2,1,0:T(8,128)(2,1)}, u32[]{:S(2)}) copy-start(bf16[1,256,4096]{2,1,0:T(8,128)(2,1)} %get-tuple-element.11) | copy-start | bytes 6291460

commit v3 on v2

--- a/solution.py
+++ b/solution.py
@@ -75,17 +75,17 @@
     def greet(rr, zz):
         pl.semaphore_signal(barrier, inc=1, device_id=(rr, zz), device_id_type=MESH)
 
-    @pl.loop(1, NZ)
+    @pl.loop(1, NZ, unroll=True)
     def _(k):
         greet(r, lax.rem(z + k, NZ))
 
-    @pl.loop(1, NS)
+    @pl.loop(1, NS, unroll=True)
     def _(k):
         greet(lax.rem(r + k, NS), z)
 
     @pl.when(source != z)
     def _():
-        @pl.loop(1, NS)
+        @pl.loop(1, NS, unroll=True)
         def _(k):
             greet(lax.rem(r + k, NS), source)
 
@@ -108,7 +108,7 @@
         pltpu.make_async_copy(ref, ref, send_sem.at[phase]).wait()
 
     def scatter(piece, place, phase):
-        @pl.loop(0, NS)
+        @pl.loop(0, NS, unroll=True)
         def _(k):
             e, qq = lax.rem(z + 1 + k // 4, NZ), lax.rem(r + k, 4)
             rr = z * 4 + qq
@@ -132,7 +132,7 @@
     extra = jnp.where(source == z, 3 * (NZ - 1), 4 * (NZ - 1))
     pl.semaphore_wait(barrier, NZ - 1 + NS - 1 + extra)
 
-    @pl.loop(1, NZ)
+    @pl.loop(1, NZ, unroll=True)
     def _(k):
         zz = lax.rem(z + k, NZ)
         remote(asend.at[zz], arecv.at[z], 0, r, zz).start()
@@ -144,7 +144,7 @@
         total = total + arecv[k]
     logit[z] = total
 
-    @pl.loop(1, NZ)
+    @pl.loop(1, NZ, unroll=True)
     def _(k):
         zz = lax.rem(z + k, NZ)
         remote(logit.at[z], logit.at[z], 1, r, zz).start()
@@ -223,7 +223,7 @@
     drows = pl.ds(pl.multiple_of(q * 16, 16), 16)
     dlanes = pl.ds(pl.multiple_of(source * LANE, LANE), LANE)
 
-    @pl.loop(1, NS)
+    @pl.loop(1, NS, unroll=True)
     def _(k):
         remote(dsend, drecv.at[drows, dlanes], 3, lax.rem(r + k, NS), z).start()
 
@@ -298,7 +298,7 @@
     frows = pl.ds(pl.multiple_of(source * 16, 16), 16)
     flanes = pl.ds(pl.multiple_of(q * LANE, LANE), LANE)
 
-    @pl.loop(1, NS)
+    @pl.loop(1, NS, unroll=True)
     def _(k):
         remote(fsend, frecv.at[frows, flanes], 5, lax.rem(r + k, NS), z).start()
 
@@ -324,7 +324,7 @@
             gsend[i * 4 + b, 0:16] = comb_part[:, lanes]
             gsend[i * 4 + b, 16:32] = disp_part[:, lanes]
 
-    @pl.loop(1, NZ)
+    @pl.loop(1, NZ, unroll=True)
     def _(k):
         zz = lax.rem(z + k, NZ)
         remote(gsend.at[zz], grecv.at[z], 6, r, zz).start()
@@ -344,7 +344,7 @@
     row_dots = jnp.sum(combine * comb_grad, axis=0, keepdims=True)
     hbuf[z] = (combine * (comb_grad - row_dots) + dispatch * (disp_grad - col_dots)).astype(BF16)
 
-    @pl.loop(1, NZ)
+    @pl.loop(1, NZ, unroll=True)
     def _(k):
         zz = lax.rem(z + k, NZ)
         remote(hbuf.at[z], hbuf.at[z], 7, r, zz).start()
@@ -362,7 +362,7 @@
         half, c = u // 4, u % 4
         isend[u] = phi_part[half * 8 : half * 8 + 8, c * LANE : (c + 1) * LANE]
 
-    @pl.loop(0, 8)
+    @pl.loop(0, 8, unroll=True)
     def _(u):
         @pl.when(4 * u != r)
         def _():
@@ -386,7 +386,7 @@
             total = total + irecv[k]
         jbuf[tile] = total * (1.0 / math.sqrt(2 * 512 * NS))
 
-        @pl.loop(1, NS)
+        @pl.loop(1, NS, unroll=True)
         def _(k):
             remote(jbuf.at[tile], jbuf.at[tile], 9, lax.rem(r + k, NS), z).start()
 
@@ -426,18 +426,42 @@
         store.wait()
 
 
+def store_kernel(gp, gphi, gwi, gwo, gp_out, gphi_out, gwi_out, gwo_out, sem):
+    pieces = [(gphi, gphi_out)]
+    for k in range(4):
+        rows = pl.ds(k * 1024, 1024)
+        pieces.append((gwi.at[:, rows], gwi_out.at[:, rows]))
+        rows = pl.ds(k * 64, 64)
+        pieces.append((gwo.at[:, rows], gwo_out.at[:, rows]))
+    for k in range(2):
+        pieces.append((gp.at[k], gp_out.at[k]))
+    copies = [
+        pltpu.make_async_copy(src, dst, sem.at[k]) for k, (src, dst) in enumerate(pieces)
+    ]
+    for copy in copies:
+        copy.start()
+    for copy in copies:
+        copy.wait()
+
+
 def local(patches, grad_out, phi_t, w_in, w_out):
     anywhere = pl.BlockSpec(memory_space=pl.ANY)
+    hbm = pl.BlockSpec(memory_space=pltpu.HBM)
+
+    def held(arrays, space):
+        return [pltpu.with_memory_space_constraint(a, space) for a in arrays]
+
     vmem = pltpu.VMEM
-    return pl.pallas_call(
+    shapes = (
+        jax.ShapeDtypeStruct(patches.shape, BF16),
+        jax.ShapeDtypeStruct(phi_t.shape, F32),
+        jax.ShapeDtypeStruct(w_in.shape, BF16),
+        jax.ShapeDtypeStruct(w_out.shape, BF16),
+    )
+    results = pl.pallas_call(
         kernel,
-        out_shape=(
-            jax.ShapeDtypeStruct(patches.shape, BF16),
-            jax.ShapeDtypeStruct(phi_t.shape, F32),
-            jax.ShapeDtypeStruct(w_in.shape, BF16),
-            jax.ShapeDtypeStruct(w_out.shape, BF16),
-        ),
-        in_specs=[anywhere] * 5,
+        out_shape=shapes,
+        in_specs=[hbm] * 5,
         out_specs=[anywhere] * 4,
         scratch_shapes=[
             vmem((2, 512, 512), BF16),
@@ -477,12 +501,20 @@
             pltpu.SemaphoreType.DMA((10,)),
         ],
         compiler_params=pltpu.CompilerParams(
-            collective_id=0, has_side_effects=True, vmem_limit_bytes=48 * 1024 * 1024
+            collective_id=0, has_side_effects=True, vmem_limit_bytes=28 * 1024 * 1024
         ),
         cost_estimate=pl.CostEstimate(
             flops=400_000_000, bytes_accessed=12_000_000, transcendentals=100_000
         ),
-    )(patches, grad_out, phi_t, w_in, w_out)
+    )(*held((patches, grad_out, phi_t, w_in, w_out), pltpu.HBM))
+    return pl.pallas_call(
+        store_kernel,
+        out_shape=shapes,
+        in_specs=[anywhere] * 4,
+        out_specs=[hbm] * 4,
+        scratch_shapes=[pltpu.SemaphoreType.DMA((11,))],
+        compiler_params=pltpu.CompilerParams(vmem_limit_bytes=4 * 1024 * 1024),
+    )(*held(results, pltpu.VMEM))
 
 
 def solution(mesh):

time: 84.8 us -> 77.6 us (0.915)
  local copies, waits for them, and re-layouts: 8.41 us -> 0 us
  Pallas kernels: 75.4 us -> 76.8 us
    unnamed x12 -> x0, local copies, waits for them, and re-layouts: 8.41 us -> none
    pallas_call x1 -> x2, Pallas kernels: 75.4 us -> 76.8 us  [the longest x1 74.3 us: local(): pl.pallas_call(kernel, out_shape=shapes, in_specs=[hbm] * 5, out_specs=[a...]
where the time goes in v3:
time: 77.6 us; the launch traced here: 77.4 us
  Pallas kernels  76.8 us (99%)
    pallas_call x1, Pallas kernels, local(): pl.pallas_call(kernel, out_shape=shapes, in_specs=[hbm] * 5, out_specs=[a...  74.3 us
    pallas_call x1, Pallas kernels, local(): pl.pallas_call(store_kernel, out_shape=shapes, in_specs=[anywhere] * 4, o...  2.44 us

profile of v3, /device:TPU:1, one launch (start us, length us, event | category | flops | bytes accessed | tf_op | source)
XLA Modules:
  0.0 77.4 jit_solution(11814591664806130967)
XLA Ops:
  0.6 74.3 %shard_map.84 = (bf16[2,512,512]{2,1,0:T(8,128)(2,1)S(1)}, f32[16,512]{1,0:T(8,128)S(1)}, bf16[1,4096,256]{2,1,0:T(8,128)(2,1)S(1)}, bf16[1,256,4096]{2,1,0:T(8,128)(2,1)S(1)}) custom-call(bf16[2,512,512]{2,1,0:T(8,128)(2,1)} %patches.1, bf16[2,512,512]{2,1,0:T(8,128)(2,1)} %grad_out.1, bf16[16,512]{1,0:T(8,128)(2,1)} %phi_t.1, bf16[1,4096,256]{2,1,0:T(8,128)(2,1)} %w_in.1, ...), custom_call_target="tpu_custom_call" | custom-call | flops 400000000 | bytes 12000000 | tf_op jit(solution)/shard_map/pallas_call | solution.py:461
  75.0 2.4 %shard_map.85 = (bf16[2,512,512]{2,1,0:T(8,128)(2,1)}, f32[16,512]{1,0:T(8,128)}, bf16[1,4096,256]{2,1,0:T(8,128)(2,1)}, bf16[1,256,4096]{2,1,0:T(8,128)(2,1)}) custom-call(bf16[2,512,512]{2,1,0:T(8,128)(2,1)S(1)} %get-tuple-element.8.gp, f32[16,512]{1,0:T(8,128)S(1)} %get-tuple-element.9.gphi, bf16[1,4096,256]{2,1,0:T(8,128)(2,1)S(1)} %get-tuple-element.10.gwi, ...), custom_call_target="tpu_custom_call" | custom-call | tf_op jit(solution)/shard_map/pallas_call | solution.py:510

commit v4 on v3

--- a/solution.py
+++ b/solution.py
@@ -19,6 +19,17 @@
 LANE = 128
 
 
+def ring(d, n):
+    return min(d, n - d)
+
+
+ALONG_EXP = sorted(range(1, NZ), key=lambda d: -ring(d, NZ))
+CHIPS = sorted(
+    ((dy, dx) for dy in range(4) for dx in range(4)), key=lambda d: -ring(d[0], 4) - ring(d[1], 4)
+)
+ALONG_SEQ = [(dy, dx, dc) for dy, dx in CHIPS for dc in range(2) if (dy, dx, dc) != (0, 0, 0)]
+
+
 def nn(a, b):
     return lax.dot_general(a, b, (((1,), (0,)), ((), ())), preferred_element_type=F32)
 
@@ -52,14 +63,19 @@
 def kernel(
     patches, grad_out, phi_t, w_in, w_out,
     grad_patches, grad_phi, grad_w_in, grad_w_out,
-    pv, gv, phv, wiv, wov, gpv, gphv, gwiv, gwov,
+    pv, gv, phv, wiv, wov,
     asend, arecv, logit, cfull, csend, crecv, dtmp, dsend, drecv, rows_f,
-    esend, erecv, fsend, frecv, lse_b, dots_b, gsend, grecv, hbuf, isend, irecv, jbuf,
-    in_sem, out_sem, send_sem, recv_sem,
+    esend, erecv, fsend, frecv, lse_b, dots_b, gsend, grecv, hbuf, pair, paired, isend, irecv, halves,
+    in_sem, send_sem, recv_sem,
 ):
     r = lax.axis_index("seq")
     z = lax.axis_index("exp")
     source, q = r // 4, lax.rem(r, 4)
+
+    y, x, core = r // 8, lax.rem(r // 2, 4), lax.rem(r, 2)
+
+    def at_offset(dy, dx, dc):
+        return (lax.rem(y + dy, 4) * 4 + lax.rem(x + dx, 4)) * 2 + lax.rem(core + dc, 2)
 
     loads = [
         pltpu.make_async_copy(src, dst, in_sem.at[k])
@@ -75,17 +91,17 @@
     def greet(rr, zz):
         pl.semaphore_signal(barrier, inc=1, device_id=(rr, zz), device_id_type=MESH)
 
-    @pl.loop(1, NZ, unroll=True)
+    @pl.loop(1, NZ)
     def _(k):
         greet(r, lax.rem(z + k, NZ))
 
-    @pl.loop(1, NS, unroll=True)
+    @pl.loop(1, NS)
     def _(k):
         greet(lax.rem(r + k, NS), z)
 
     @pl.when(source != z)
     def _():
-        @pl.loop(1, NS, unroll=True)
+        @pl.loop(1, NS)
         def _(k):
             greet(lax.rem(r + k, NS), source)
 
@@ -108,18 +124,22 @@
         pltpu.make_async_copy(ref, ref, send_sem.at[phase]).wait()
 
     def scatter(piece, place, phase):
-        @pl.loop(0, NS, unroll=True)
-        def _(k):
-            e, qq = lax.rem(z + 1 + k // 4, NZ), lax.rem(r + k, 4)
+        for d in ALONG_EXP:
+            e = lax.rem(z + d, NZ)
+            for k in range(4):
+                qq = lax.rem(r + k, 4)
+                remote(piece(qq, e), place, phase, z * 4 + qq, e).start()
+        for k in range(4):
+            qq = lax.rem(r + k, 4)
             rr = z * 4 + qq
 
-            @pl.when((rr != r) | (e != z))
+            @pl.when(rr != r)
             def _():
-                remote(piece(qq, e), place, phase, rr, e).start()
-
-            @pl.when((rr == r) & (e == z))
+                remote(piece(qq, z), place, phase, rr, z).start()
+
+            @pl.when(rr == r)
             def _():
-                pltpu.make_async_copy(piece(qq, e), place, recv_sem.at[phase]).start()
+                pltpu.make_async_copy(piece(qq, z), place, recv_sem.at[phase]).start()
 
     loads[0].wait()
     loads[1].wait()
@@ -132,9 +152,8 @@
     extra = jnp.where(source == z, 3 * (NZ - 1), 4 * (NZ - 1))
     pl.semaphore_wait(barrier, NZ - 1 + NS - 1 + extra)
 
-    @pl.loop(1, NZ, unroll=True)
-    def _(k):
-        zz = lax.rem(z + k, NZ)
+    for d in ALONG_EXP:
+        zz = lax.rem(z + d, NZ)
         remote(asend.at[zz], arecv.at[z], 0, r, zz).start()
 
     arecv[z] = asend[z]
@@ -144,9 +163,8 @@
         total = total + arecv[k]
     logit[z] = total
 
-    @pl.loop(1, NZ, unroll=True)
-    def _(k):
-        zz = lax.rem(z + k, NZ)
+    for d in ALONG_EXP:
+        zz = lax.rem(z + d, NZ)
         remote(logit.at[z], logit.at[z], 1, r, zz).start()
 
     arrived(logit.at[pl.ds(0, NZ - 1)], 1)
@@ -223,9 +241,8 @@
     drows = pl.ds(pl.multiple_of(q * 16, 16), 16)
     dlanes = pl.ds(pl.multiple_of(source * LANE, LANE), LANE)
 
-    @pl.loop(1, NS, unroll=True)
-    def _(k):
-        remote(dsend, drecv.at[drows, dlanes], 3, lax.rem(r + k, NS), z).start()
+    for d in ALONG_SEQ:
+        remote(dsend, drecv.at[drows, dlanes], 3, at_offset(*d), z).start()
 
     drecv[drows, dlanes] = dsend[...]
 
@@ -275,14 +292,8 @@
 
     scatter(block, erecv.at[r], 4)
 
-    gwov[0] = tn(active_hi, lhs).astype(BF16)
-    gwiv[0] = tn(lhs, pre_lo).astype(BF16)
-    stores = [
-        pltpu.make_async_copy(gwiv, grad_w_in, out_sem.at[0]),
-        pltpu.make_async_copy(gwov, grad_w_out, out_sem.at[1]),
-    ]
-    for store in stores:
-        store.start()
+    grad_w_out[0] = tn(active_hi, lhs).astype(BF16)
+    grad_w_in[0] = tn(lhs, pre_lo).astype(BF16)
 
     arrived(erecv, 4)
     total = erecv[0].astype(F32)
@@ -298,9 +309,8 @@
     frows = pl.ds(pl.multiple_of(source * 16, 16), 16)
     flanes = pl.ds(pl.multiple_of(q * LANE, LANE), LANE)
 
-    @pl.loop(1, NS, unroll=True)
-    def _(k):
-        remote(fsend, frecv.at[frows, flanes], 5, lax.rem(r + k, NS), z).start()
+    for d in ALONG_SEQ:
+        remote(fsend, frecv.at[frows, flanes], 5, at_offset(*d), z).start()
 
     frecv[frows, flanes] = fsend[...]
 
@@ -321,12 +331,11 @@
         disp_part = nt(input_grad[rows], pv[i])
         for b in range(4):
             lanes = slice(b * LANE, (b + 1) * LANE)
-            gsend[i * 4 + b, 0:16] = comb_part[:, lanes]
-            gsend[i * 4 + b, 16:32] = disp_part[:, lanes]
-
-    @pl.loop(1, NZ, unroll=True)
-    def _(k):
-        zz = lax.rem(z + k, NZ)
+            gsend[i * 4 + b, 0:16] = comb_part[:, lanes].astype(BF16)
+            gsend[i * 4 + b, 16:32] = disp_part[:, lanes].astype(BF16)
+
+    for d in ALONG_EXP:
+        zz = lax.rem(z + d, NZ)
         remote(gsend.at[zz], grecv.at[z], 6, r, zz).start()
 
     grecv[z] = gsend[z]
@@ -337,16 +346,15 @@
     dispatch = jnp.exp(chunk - lse_b[image, :])
     col_dots = dots_b[image, :]
     arrived(grecv.at[pl.ds(0, NZ - 1)], 6)
-    total = grecv[0]
+    total = grecv[0].astype(F32)
     for k in range(1, NZ):
-        total = total + grecv[k]
+        total = total + grecv[k].astype(F32)
     comb_grad, disp_grad = total[0:16], total[16:32]
     row_dots = jnp.sum(combine * comb_grad, axis=0, keepdims=True)
     hbuf[z] = (combine * (comb_grad - row_dots) + dispatch * (disp_grad - col_dots)).astype(BF16)
 
-    @pl.loop(1, NZ, unroll=True)
-    def _(k):
-        zz = lax.rem(z + k, NZ)
+    for d in ALONG_EXP:
+        zz = lax.rem(z + d, NZ)
         remote(hbuf.at[z], hbuf.at[z], 7, r, zz).start()
 
     dispatch_b = []
@@ -358,59 +366,41 @@
         jnp.concatenate([hbuf[i * 4 + b] for b in range(4)], axis=1) for i in range(2)
     ]
     phi_part = nn(logit_b[0], pv[0]) + nn(logit_b[1], pv[1])
-    for u in range(8):
-        half, c = u // 4, u % 4
-        isend[u] = phi_part[half * 8 : half * 8 + 8, c * LANE : (c + 1) * LANE]
-
-    @pl.loop(0, 8, unroll=True)
-    def _(u):
-        @pl.when(4 * u != r)
-        def _():
-            remote(isend.at[u], irecv.at[r], 8, 4 * u, z).start()
-
-    for i in range(2):
+    for h in range(2):
+        slots = slice(h * 8, h * 8 + 8)
+        pair[h] = jnp.concatenate([phi_part[slots, 0:256], phi_part[slots, 256:512]], axis=0)
+
+    def spread_patches(i):
         left = jnp.concatenate([dispatch_b[i], logit_b[i]], axis=0)
         right = jnp.concatenate([input_grad[i * 16 : i * 16 + 16], phi], axis=0)
-        gpv[i] = tn(left, right).astype(BF16)
-    stores.append(pltpu.make_async_copy(gpv, grad_patches, out_sem.at[2]))
-    stores[2].start()
-
-    tile = r // 4
-
-    @pl.when(lax.rem(r, 4) == 0)
-    def _():
-        irecv[r] = isend[tile]
-        arrived(irecv.at[pl.ds(0, NS - 1)], 8)
-        total = irecv[0]
-        for k in range(1, NS):
-            total = total + irecv[k]
-        jbuf[tile] = total * (1.0 / math.sqrt(2 * 512 * NS))
-
-        @pl.loop(1, NS, unroll=True)
-        def _(k):
-            remote(jbuf.at[tile], jbuf.at[tile], 9, lax.rem(r + k, NS), z).start()
-
-        arrived(jbuf.at[pl.ds(0, 7)], 9)
-        sent(irecv.at[pl.ds(0, NS - 1)], 9)
-        sent(isend.at[pl.ds(0, 7)], 8)
-
-    @pl.when(lax.rem(r, 4) != 0)
-    def _():
-        arrived(jbuf, 9)
-        sent(isend, 8)
-
-    for u in range(8):
-        half, c = u // 4, u % 4
-        gphv[half * 8 : half * 8 + 8, c * LANE : (c + 1) * LANE] = jbuf[u]
-    stores.append(pltpu.make_async_copy(gphv, grad_phi, out_sem.at[3]))
-    stores[3].start()
-
+        grad_patches[i] = tn(left, right).astype(BF16)
+
+    sibling = at_offset(0, 0, 1)
+    trade = remote(pair.at[1 - core], paired, 8, sibling, z)
+    trade.start()
+    spread_patches(0)
+    trade.wait_recv()
+    half_sum = pair[core] + paired[...]
+    isend[...] = half_sum.astype(BF16)
+    for dy, dx in CHIPS[:-1]:
+        remote(isend, irecv.at[r // 2], 9, at_offset(dy, dx, 0), z).start()
+    irecv[r // 2] = isend[...]
+    spread_patches(1)
+    arrived(irecv.at[pl.ds(0, 15)], 9)
+    total = irecv[0].astype(F32)
+    for k in range(1, 16):
+        total = total + irecv[k].astype(F32)
+    halves[core] = total * (1.0 / math.sqrt(2 * 512 * NS))
+    back = remote(halves.at[core], halves.at[core], 10, sibling, z)
+    back.start()
     sent(asend.at[pl.ds(0, NZ - 1)], 0)
     sent(logit.at[pl.ds(0, NZ - 1)], 1)
     sent(dwait, 3)
     sent(fwait, 5)
     sent(gsend.at[pl.ds(0, NZ - 1)], 6)
     sent(hbuf.at[pl.ds(0, NZ - 1)], 7)
+    trade.wait_send()
+    sent(irecv.at[pl.ds(0, 15)], 9)
 
     @pl.when(source == z)
     def _():
@@ -422,8 +412,10 @@
         sent(crecv, 2)
         sent(erecv, 4)
 
-    for store in stores:
-        store.wait()
+    back.wait()
+    for h in range(2):
+        grad_phi[h * 8 : h * 8 + 8, 0:256] = halves[h, 0:8]
+        grad_phi[h * 8 : h * 8 + 8, 256:512] = halves[h, 8:16]
 
 
 def store_kernel(gp, gphi, gwi, gwo, gp_out, gphi_out, gwi_out, gwo_out, sem):
@@ -462,15 +454,11 @@
         kernel,
         out_shape=shapes,
         in_specs=[hbm] * 5,
-        out_specs=[anywhere] * 4,
+        out_specs=[pl.BlockSpec(memory_space=pltpu.VMEM)] * 4,
         scratch_shapes=[
             vmem((2, 512, 512), BF16),
             vmem((2, 512, 512), BF16),
             vmem((16, 512), BF16),
-            vmem((1, 4096, 256), BF16),
-            vmem((1, 256, 4096), BF16),
-            vmem((2, 512, 512), BF16),
-            vmem((16, 512), F32),
             vmem((1, 4096, 256), BF16),
             vmem((1, 256, 4096), BF16),
             vmem((8, 16, LANE), F32),
@@ -489,16 +477,17 @@
             vmem((LANE, 512), BF16),
             vmem((32, LANE), F32),
             vmem((32, LANE), F32),
-            vmem((8, 32, LANE), F32),
-            vmem((8, 32, LANE), F32),
+            vmem((8, 32, LANE), BF16),
+            vmem((8, 32, LANE), BF16),
             vmem((8, 16, LANE), BF16),
-            vmem((8, 8, LANE), F32),
-            vmem((32, 8, LANE), F32),
-            vmem((8, 8, LANE), F32),
+            vmem((2, 16, 256), F32),
+            vmem((16, 256), F32),
+            vmem((16, 256), BF16),
+            vmem((16, 16, 256), BF16),
+            vmem((2, 16, 256), F32),
             pltpu.SemaphoreType.DMA((5,)),
-            pltpu.SemaphoreType.DMA((4,)),
-            pltpu.SemaphoreType.DMA((10,)),
-            pltpu.SemaphoreType.DMA((10,)),
+            pltpu.SemaphoreType.DMA((11,)),
+            pltpu.SemaphoreType.DMA((11,)),
         ],
         compiler_params=pltpu.CompilerParams(
             collective_id=0, has_side_effects=True, vmem_limit_bytes=28 * 1024 * 1024

time: 77.6 us -> 70.2 us (0.905)
  Pallas kernels: 76.8 us -> 69.4 us
    pallas_call x1, Pallas kernels: 74.3 us -> 66.9 us  [local(): pl.pallas_call(kernel, out_shape=shapes, in_specs=[hbm] * 5, out_specs=[p...]
where the time goes in v4:
time: 70.2 us; the launch traced here: 70 us
  Pallas kernels  69.4 us (99%)
    pallas_call x1, Pallas kernels, local(): pl.pallas_call(kernel, out_shape=shapes, in_specs=[hbm] * 5, out_specs=[p...  66.9 us
    pallas_call x1, Pallas kernels, local(): pl.pallas_call(store_kernel, out_shape=shapes, in_specs=[anywhere] * 4, o...  2.44 us

profile of v4, /device:TPU:1, one launch (start us, length us, event | category | flops | bytes accessed | tf_op | source)
XLA Modules:
  0.0 70.0 jit_solution(11917349969014031243)
XLA Ops:
  0.6 66.9 %shard_map.84 = (bf16[2,512,512]{2,1,0:T(8,128)(2,1)S(1)}, f32[16,512]{1,0:T(8,128)S(1)}, bf16[1,4096,256]{2,1,0:T(8,128)(2,1)S(1)}, bf16[1,256,4096]{2,1,0:T(8,128)(2,1)S(1)}) custom-call(bf16[2,512,512]{2,1,0:T(8,128)(2,1)} %patches.1, bf16[2,512,512]{2,1,0:T(8,128)(2,1)} %grad_out.1, bf16[16,512]{1,0:T(8,128)(2,1)} %phi_t.1, bf16[1,4096,256]{2,1,0:T(8,128)(2,1)} %w_in.1, ...), custom_call_target="tpu_custom_call" | custom-call | flops 400000000 | bytes 12000000 | tf_op jit(solution)/shard_map/pallas_call | solution.py:453
  67.6 2.4 %shard_map.85 = (bf16[2,512,512]{2,1,0:T(8,128)(2,1)}, f32[16,512]{1,0:T(8,128)}, bf16[1,4096,256]{2,1,0:T(8,128)(2,1)}, bf16[1,256,4096]{2,1,0:T(8,128)(2,1)}) custom-call(bf16[2,512,512]{2,1,0:T(8,128)(2,1)S(1)} %get-tuple-element.8.gp, f32[16,512]{1,0:T(8,128)S(1)} %get-tuple-element.9.gphi, bf16[1,4096,256]{2,1,0:T(8,128)(2,1)S(1)} %get-tuple-element.10.gwi, ...), custom_call_target="tpu_custom_call" | custom-call | tf_op jit(solution)/shard_map/pallas_call | solution.py:499

commit v5 on v4

--- a/solution.py
+++ b/solution.py
@@ -63,10 +63,10 @@
 def kernel(
     patches, grad_out, phi_t, w_in, w_out,
     grad_patches, grad_phi, grad_w_in, grad_w_out,
-    pv, gv, phv, wiv, wov,
+    pv, gv, phv, wiv, wov, pvt, gvt, wit, wot,
     asend, arecv, logit, cfull, csend, crecv, dtmp, dsend, drecv, rows_f,
-    esend, erecv, fsend, frecv, lse_b, dots_b, gsend, grecv, hbuf, pair, paired, isend, irecv, halves,
-    in_sem, send_sem, recv_sem,
+    esend, erecv, fsend, frecv, lse_b, dots_b, gsend, grecv, hbuf, pair, paired, isend, irecv,
+    in_sem, send_sem, recv_sem, d_sem, known,
 ):
     r = lax.axis_index("seq")
     z = lax.axis_index("exp")
@@ -80,10 +80,13 @@
     loads = [
         pltpu.make_async_copy(src, dst, in_sem.at[k])
         for k, (src, dst) in enumerate(
-            [(phi_t, phv), (patches, pv), (grad_out, gv), (w_in, wiv), (w_out, wov)]
+            [
+                (phi_t, phv), (patches.at[0], pv.at[0]), (patches.at[1], pv.at[1]),
+                (grad_out, gv), (w_out, wov), (w_in, wiv),
+            ]
         )
     ]
-    for load in loads:
+    for load in loads[:3]:
         load.start()
 
     barrier = pltpu.get_barrier_semaphore()
@@ -91,19 +94,18 @@
     def greet(rr, zz):
         pl.semaphore_signal(barrier, inc=1, device_id=(rr, zz), device_id_type=MESH)
 
-    @pl.loop(1, NZ)
-    def _(k):
-        greet(r, lax.rem(z + k, NZ))
-
-    @pl.loop(1, NS)
-    def _(k):
-        greet(lax.rem(r + k, NS), z)
-
-    @pl.when(source != z)
-    def _():
-        @pl.loop(1, NS)
-        def _(k):
-            greet(lax.rem(r + k, NS), source)
+    x_line = [at_offset(0, d, 0) for d in (2, 1, 3)]
+    y_line = [at_offset(d, 0, 0) for d in (2, 1, 3)]
+    sibling = at_offset(0, 0, 1)
+
+    for d in ALONG_EXP:
+        greet(r, lax.rem(z + d, NZ))
+    for rr in x_line + y_line + [sibling]:
+        greet(rr, z)
+
+    def tell(line, step):
+        for rr in line:
+            pl.semaphore_signal(known.at[step], inc=1, device_id=(rr, z), device_id_type=MESH)
 
     def remote(src, dst, phase, rr, zz):
         return pltpu.make_async_remote_copy(
@@ -142,21 +144,27 @@
                 pltpu.make_async_copy(piece(qq, z), place, recv_sem.at[phase]).start()
 
     loads[0].wait()
-    loads[1].wait()
     phi = phv[...]
     for i in range(2):
+        loads[1 + i].wait()
         part = nt(phi, pv[i])
         for b in range(4):
             asend[i * 4 + b] = part[:, b * LANE : (b + 1) * LANE]
-
-    extra = jnp.where(source == z, 3 * (NZ - 1), 4 * (NZ - 1))
-    pl.semaphore_wait(barrier, NZ - 1 + NS - 1 + extra)
+    for load in loads[3:]:
+        load.start()
+
+    pl.semaphore_wait(barrier, NZ - 1 + 7)
 
     for d in ALONG_EXP:
         zz = lax.rem(z + d, NZ)
         remote(asend.at[zz], arecv.at[z], 0, r, zz).start()
 
     arecv[z] = asend[z]
+    tell([sibling], 0)
+    pl.semaphore_wait(known.at[0], 1)
+    tell(x_line, 1)
+    loads[4].wait()
+    wot[...] = wov[0].T
     arrived(arecv.at[pl.ds(0, NZ - 1)], 0)
     total = arecv[0]
     for k in range(1, NZ):
@@ -167,8 +175,13 @@
         zz = lax.rem(z + d, NZ)
         remote(logit.at[z], logit.at[z], 1, r, zz).start()
 
+    pl.semaphore_wait(known.at[1], 3)
+    tell(y_line, 2)
+    loads[5].wait()
+    wit[...] = wiv[0].T
+    loads[3].wait()
     arrived(logit.at[pl.ds(0, NZ - 1)], 1)
-    loads[2].wait()
+    pl.semaphore_wait(known.at[2], 3)
 
     diag = iota((32, LANE), 0) == iota((32, LANE), 1)
     peaks, sums = [], []
@@ -208,6 +221,9 @@
         return csend.at[pl.ds(pl.multiple_of(row * 16, 16), 16)]
 
     scatter(piece, crecv.at[pl.ds(pl.multiple_of(r * 16, 16), 16)], 2)
+    for i in range(2):
+        pvt[i] = pv[i].T
+        gvt[i] = gv[i].T
     arrived(crecv, 2)
     cfull[...] = crecv[...].astype(F32)
     peak_all = cfull[pl.ds(12, 32, stride=16), :]
@@ -241,8 +257,15 @@
     drows = pl.ds(pl.multiple_of(q * 16, 16), 16)
     dlanes = pl.ds(pl.multiple_of(source * LANE, LANE), LANE)
 
-    for d in ALONG_SEQ:
-        remote(dsend, drecv.at[drows, dlanes], 3, at_offset(*d), z).start()
+    for dy, dx, dc in ALONG_SEQ:
+        pltpu.make_async_remote_copy(
+            src_ref=dsend,
+            dst_ref=drecv.at[drows, dlanes],
+            send_sem=send_sem.at[3],
+            recv_sem=d_sem.at[(4 - dy) % 4],
+            device_id=(at_offset(dy, dx, dc), z),
+            device_id_type=MESH,
+        ).start()
 
     drecv[drows, dlanes] = dsend[...]
 
@@ -252,18 +275,25 @@
     want = lax.rem(j, 4) * 16 + part_of + c_of
     pick = jnp.where(iota((96, 64), 1) == want, 1.0, 0.0).astype(BF16)
 
-    arrived(dwait, 3)
-    picked = nn(pick, drecv[...])
-    for c in range(4):
-        for b in range(NZ):
-            rows_f[:, (b * 4 + c) * LANE : (b * 4 + c + 1) * LANE] = picked[
-                c * 24 : c * 24 + 24, b * LANE : (b + 1) * LANE
-            ]
-    loads[3].wait()
-    loads[4].wait()
+    hidden = act_grad = None
+    for g in (0, 1, 3, 2):
+        come = csend.at[pl.ds(0, 16 * (7 if g == 0 else 8))]
+        pltpu.make_async_copy(come, come, d_sem.at[g]).wait()
+        first = lax.rem(y + g, 4) * 2
+        lanes = pl.ds(pl.multiple_of(first * LANE, 2 * LANE), 2 * LANE)
+        picked = nn(pick, drecv[:, lanes])
+        strips = []
+        for b in range(2):
+            for c in range(4):
+                strips.append(picked[c * 24 : c * 24 + 24, b * LANE : (b + 1) * LANE])
+        strip = jnp.concatenate(strips, axis=1)
+        features = pl.ds(pl.multiple_of(first * 512, 1024), 1024)
+        rows_f[:, features] = strip
+        left = strip[0:16].astype(BF16)
+        h, a = nn(left, wiv[0, features, :]), nn(left, wot[features, :])
+        hidden, act_grad = (h, a) if hidden is None else (hidden + h, act_grad + a)
+    hidden, act_grad = hidden[0:8], act_grad[8:16]
     lhs = rows_f[0:16, :].astype(BF16)
-    hidden = nn(lhs, wiv[0])[0:8]
-    act_grad = nt(lhs, wov[0])[8:16]
     inner = slope_coef * (hidden + cubic_coef * hidden * hidden * hidden)
     tangent = jnp.tanh(inner)
     active = 0.5 * hidden * (1.0 + tangent)
@@ -278,7 +308,7 @@
     active_lo = jnp.concatenate([active, none], axis=0).astype(BF16)
     active_hi = jnp.concatenate([none, active], axis=0).astype(BF16)
     pre_lo = jnp.concatenate([pre, none], axis=0).astype(BF16)
-    result = (nn(active_lo, wov[0]) + nt(pre_lo, wiv[0]))[0:8]
+    result = (nn(active_lo, wov[0]) + nn(pre_lo, wit[...]))[0:8]
     wide = iota((8, 4096), 0) < 4
     dots = jnp.sum(result * (rows_f[0:8, :] + rows_f[16:24, :]), axis=1, keepdims=True)
     high = result.astype(BF16).astype(F32)
@@ -327,8 +357,8 @@
     dots_b[...] = jnp.broadcast_to(jnp.sum(picked[64:96, 0:LANE], axis=1, keepdims=True), (32, LANE))
     for i in range(2):
         rows = slice(i * 16, i * 16 + 16)
-        comb_part = nt(slot_out[rows], gv[i])
-        disp_part = nt(input_grad[rows], pv[i])
+        comb_part = nn(slot_out[rows], gvt[i])
+        disp_part = nn(input_grad[rows], pvt[i])
         for b in range(4):
             lanes = slice(b * LANE, (b + 1) * LANE)
             gsend[i * 4 + b, 0:16] = comb_part[:, lanes].astype(BF16)
@@ -375,24 +405,24 @@
         right = jnp.concatenate([input_grad[i * 16 : i * 16 + 16], phi], axis=0)
         grad_patches[i] = tn(left, right).astype(BF16)
 
-    sibling = at_offset(0, 0, 1)
     trade = remote(pair.at[1 - core], paired, 8, sibling, z)
     trade.start()
     spread_patches(0)
     trade.wait_recv()
     half_sum = pair[core] + paired[...]
     isend[...] = half_sum.astype(BF16)
-    for dy, dx in CHIPS[:-1]:
-        remote(isend, irecv.at[r // 2], 9, at_offset(dy, dx, 0), z).start()
-    irecv[r // 2] = isend[...]
+    for d in ALONG_SEQ:
+        remote(isend, irecv.at[r], 9, at_offset(*d), z).start()
+    irecv[r] = isend[...]
     spread_patches(1)
-    arrived(irecv.at[pl.ds(0, 15)], 9)
-    total = irecv[0].astype(F32)
-    for k in range(1, 16):
-        total = total + irecv[k].astype(F32)
-    halves[core] = total * (1.0 / math.sqrt(2 * 512 * NS))
-    back = remote(halves.at[core], halves.at[core], 10, sibling, z)
-    back.start()
+    arrived(irecv.at[pl.ds(0, NS - 1)], 9)
+    for h in range(2):
+        total = irecv[h].astype(F32)
+        for k in range(1, 16):
+            total = total + irecv[2 * k + h].astype(F32)
+        total = total * (1.0 / math.sqrt(2 * 512 * NS))
+        grad_phi[h * 8 : h * 8 + 8, 0:256] = total[0:8]
+        grad_phi[h * 8 : h * 8 + 8, 256:512] = total[8:16]
     sent(asend.at[pl.ds(0, NZ - 1)], 0)
     sent(logit.at[pl.ds(0, NZ - 1)], 1)
     sent(dwait, 3)
@@ -400,7 +430,7 @@
     sent(gsend.at[pl.ds(0, NZ - 1)], 6)
     sent(hbuf.at[pl.ds(0, NZ - 1)], 7)
     trade.wait_send()
-    sent(irecv.at[pl.ds(0, 15)], 9)
+    sent(irecv.at[pl.ds(0, NS - 1)], 9)
 
     @pl.when(source == z)
     def _():
@@ -411,11 +441,6 @@
     def _():
         sent(crecv, 2)
         sent(erecv, 4)
-
-    back.wait()
-    for h in range(2):
-        grad_phi[h * 8 : h * 8 + 8, 0:256] = halves[h, 0:8]
-        grad_phi[h * 8 : h * 8 + 8, 256:512] = halves[h, 8:16]
 
 
 def store_kernel(gp, gphi, gwi, gwo, gp_out, gphi_out, gwi_out, gwo_out, sem):
@@ -461,6 +486,10 @@
             vmem((16, 512), BF16),
             vmem((1, 4096, 256), BF16),
             vmem((1, 256, 4096), BF16),
+            vmem((2, 512, 512), BF16),
+            vmem((2, 512, 512), BF16),
+            vmem((256, 4096), BF16),
+            vmem((4096, 256), BF16),
             vmem((8, 16, LANE), F32),
             vmem((8, 16, LANE), F32),
             vmem((8, 16, LANE), F32),
@@ -483,11 +512,12 @@
             vmem((2, 16, 256), F32),
             vmem((16, 256), F32),
             vmem((16, 256), BF16),
-            vmem((16, 16, 256), BF16),
-            vmem((2, 16, 256), F32),
-            pltpu.SemaphoreType.DMA((5,)),
-            pltpu.SemaphoreType.DMA((11,)),
-            pltpu.SemaphoreType.DMA((11,)),
+            vmem((32, 16, 256), BF16),
+            pltpu.SemaphoreType.DMA((6,)),
+            pltpu.SemaphoreType.DMA((10,)),
+            pltpu.SemaphoreType.DMA((10,)),
+            pltpu.SemaphoreType.DMA((4,)),
+            pltpu.SemaphoreType.REGULAR((3,)),
         ],
         compiler_params=pltpu.CompilerParams(
             collective_id=0, has_side_effects=True, vmem_limit_bytes=28 * 1024 * 1024

time: 70.2 us -> 66.6 us (0.949)
  Pallas kernels: 69.4 us -> 65.8 us
    pallas_call x1, Pallas kernels: 66.9 us -> 63.4 us  [local(): pl.pallas_call(kernel, out_shape=shapes, in_specs=[hbm] * 5, out_specs=[p...]
where the time goes in v5:
time: 66.6 us; the launch traced here: 66.5 us
  Pallas kernels  65.8 us (99%)
    pallas_call x1, Pallas kernels, local(): pl.pallas_call(kernel, out_shape=shapes, in_specs=[hbm] * 5, out_specs=[p...  63.4 us
    pallas_call x1, Pallas kernels, local(): pl.pallas_call(store_kernel, out_shape=shapes, in_specs=[anywhere] * 4, o...  2.44 us

profile of v5, /device:TPU:1, one launch (start us, length us, event | category | flops | bytes accessed | tf_op | source)
XLA Modules:
  0.0 66.5 jit_solution(15956852680214857002)
XLA Ops:
  0.6 63.4 %shard_map.84 = (bf16[2,512,512]{2,1,0:T(8,128)(2,1)S(1)}, f32[16,512]{1,0:T(8,128)S(1)}, bf16[1,4096,256]{2,1,0:T(8,128)(2,1)S(1)}, bf16[1,256,4096]{2,1,0:T(8,128)(2,1)S(1)}) custom-call(bf16[2,512,512]{2,1,0:T(8,128)(2,1)} %patches.1, bf16[2,512,512]{2,1,0:T(8,128)(2,1)} %grad_out.1, bf16[16,512]{1,0:T(8,128)(2,1)} %phi_t.1, bf16[1,4096,256]{2,1,0:T(8,128)(2,1)} %w_in.1, ...), custom_call_target="tpu_custom_call" | custom-call | flops 400000000 | bytes 12000000 | tf_op jit(solution)/shard_map/pallas_call | solution.py:478
  64.0 2.4 %shard_map.85 = (bf16[2,512,512]{2,1,0:T(8,128)(2,1)}, f32[16,512]{1,0:T(8,128)}, bf16[1,4096,256]{2,1,0:T(8,128)(2,1)}, bf16[1,256,4096]{2,1,0:T(8,128)(2,1)}) custom-call(bf16[2,512,512]{2,1,0:T(8,128)(2,1)S(1)} %get-tuple-element.8.gp, f32[16,512]{1,0:T(8,128)S(1)} %get-tuple-element.9.gphi, bf16[1,4096,256]{2,1,0:T(8,128)(2,1)S(1)} %get-tuple-element.10.gwi, ...), custom_call_target="tpu_custom_call" | custom-call | tf_op jit(solution)/shard_map/pallas_call | solution.py:529

commit v6 on v5

--- a/solution.py
+++ b/solution.py
@@ -65,7 +65,7 @@
     grad_patches, grad_phi, grad_w_in, grad_w_out,
     pv, gv, phv, wiv, wov, pvt, gvt, wit, wot,
     asend, arecv, logit, cfull, csend, crecv, dtmp, dsend, drecv, rows_f,
-    esend, erecv, fsend, frecv, lse_b, dots_b, gsend, grecv, hbuf, pair, paired, isend, irecv,
+    esend, erecv, fsend, frecv, lse_b, dots_b, gsend, grecv, hbuf, pair, paired, isend, irecv, halves,
     in_sem, send_sem, recv_sem, d_sem, known,
 ):
     r = lax.axis_index("seq")
@@ -257,7 +257,7 @@
     drows = pl.ds(pl.multiple_of(q * 16, 16), 16)
     dlanes = pl.ds(pl.multiple_of(source * LANE, LANE), LANE)
 
-    for dy, dx, dc in ALONG_SEQ:
+    for dy, dx, dc in ALONG_SEQ[::-1]:
         pltpu.make_async_remote_copy(
             src_ref=dsend,
             dst_ref=drecv.at[drows, dlanes],
@@ -339,7 +339,7 @@
     frows = pl.ds(pl.multiple_of(source * 16, 16), 16)
     flanes = pl.ds(pl.multiple_of(q * LANE, LANE), LANE)
 
-    for d in ALONG_SEQ:
+    for d in ALONG_SEQ[::-1]:
         remote(fsend, frecv.at[frows, flanes], 5, at_offset(*d), z).start()
 
     frecv[frows, flanes] = fsend[...]
@@ -411,18 +411,17 @@
     trade.wait_recv()
     half_sum = pair[core] + paired[...]
     isend[...] = half_sum.astype(BF16)
-    for d in ALONG_SEQ:
-        remote(isend, irecv.at[r], 9, at_offset(*d), z).start()
-    irecv[r] = isend[...]
+    for dy, dx in CHIPS[:-1]:
+        remote(isend, irecv.at[r // 2], 9, at_offset(dy, dx, 0), z).start()
+    irecv[r // 2] = isend[...]
     spread_patches(1)
-    arrived(irecv.at[pl.ds(0, NS - 1)], 9)
-    for h in range(2):
-        total = irecv[h].astype(F32)
-        for k in range(1, 16):
-            total = total + irecv[2 * k + h].astype(F32)
-        total = total * (1.0 / math.sqrt(2 * 512 * NS))
-        grad_phi[h * 8 : h * 8 + 8, 0:256] = total[0:8]
-        grad_phi[h * 8 : h * 8 + 8, 256:512] = total[8:16]
+    arrived(irecv.at[pl.ds(0, 15)], 9)
+    total = irecv[0].astype(F32)
+    for k in range(1, 16):
+        total = total + irecv[k].astype(F32)
+    halves[core] = total * (1.0 / math.sqrt(2 * 512 * NS))
+    back = remote(halves.at[core], halves.at[core], 10, sibling, z)
+    back.start()
     sent(asend.at[pl.ds(0, NZ - 1)], 0)
     sent(logit.at[pl.ds(0, NZ - 1)], 1)
     sent(dwait, 3)
@@ -430,7 +429,7 @@
     sent(gsend.at[pl.ds(0, NZ - 1)], 6)
     sent(hbuf.at[pl.ds(0, NZ - 1)], 7)
     trade.wait_send()
-    sent(irecv.at[pl.ds(0, NS - 1)], 9)
+    sent(irecv.at[pl.ds(0, 15)], 9)
 
     @pl.when(source == z)
     def _():
@@ -441,6 +440,11 @@
     def _():
         sent(crecv, 2)
         sent(erecv, 4)
+
+    back.wait()
+    for h in range(2):
+        grad_phi[h * 8 : h * 8 + 8, 0:256] = halves[h, 0:8]
+        grad_phi[h * 8 : h * 8 + 8, 256:512] = halves[h, 8:16]
 
 
 def store_kernel(gp, gphi, gwi, gwo, gp_out, gphi_out, gwi_out, gwo_out, sem):
@@ -512,10 +516,11 @@
             vmem((2, 16, 256), F32),
             vmem((16, 256), F32),
             vmem((16, 256), BF16),
-            vmem((32, 16, 256), BF16),
+            vmem((16, 16, 256), BF16),
+            vmem((2, 16, 256), F32),
             pltpu.SemaphoreType.DMA((6,)),
-            pltpu.SemaphoreType.DMA((10,)),
-            pltpu.SemaphoreType.DMA((10,)),
+            pltpu.SemaphoreType.DMA((11,)),
+            pltpu.SemaphoreType.DMA((11,)),
             pltpu.SemaphoreType.DMA((4,)),
             pltpu.SemaphoreType.REGULAR((3,)),
         ],

time: 66.6 us -> 66.4 us (level)
  no operation moved by 1% of the time
where the time goes in v6:
time: 66.4 us; the launch traced here: 66.2 us
  Pallas kernels  65.6 us (99%)
    pallas_call x1, Pallas kernels, local(): pl.pallas_call(kernel, out_shape=shapes, in_specs=[hbm] * 5, out_specs=[p...  63.1 us
    pallas_call x1, Pallas kernels, local(): pl.pallas_call(store_kernel, out_shape=shapes, in_specs=[anywhere] * 4, o...  2.44 us

profile of v6, /device:TPU:1, one launch (start us, length us, event | category | flops | bytes accessed | tf_op | source)
XLA Modules:
  0.0 66.2 jit_solution(9146757103153701482)
XLA Ops:
  0.6 63.1 %shard_map.84 = (bf16[2,512,512]{2,1,0:T(8,128)(2,1)S(1)}, f32[16,512]{1,0:T(8,128)S(1)}, bf16[1,4096,256]{2,1,0:T(8,128)(2,1)S(1)}, bf16[1,256,4096]{2,1,0:T(8,128)(2,1)S(1)}) custom-call(bf16[2,512,512]{2,1,0:T(8,128)(2,1)} %patches.1, bf16[2,512,512]{2,1,0:T(8,128)(2,1)} %grad_out.1, bf16[16,512]{1,0:T(8,128)(2,1)} %phi_t.1, bf16[1,4096,256]{2,1,0:T(8,128)(2,1)} %w_in.1, ...), custom_call_target="tpu_custom_call" | custom-call | flops 400000000 | bytes 12000000 | tf_op jit(solution)/shard_map/pallas_call | solution.py:482
  63.8 2.4 %shard_map.85 = (bf16[2,512,512]{2,1,0:T(8,128)(2,1)}, f32[16,512]{1,0:T(8,128)}, bf16[1,4096,256]{2,1,0:T(8,128)(2,1)}, bf16[1,256,4096]{2,1,0:T(8,128)(2,1)}) custom-call(bf16[2,512,512]{2,1,0:T(8,128)(2,1)S(1)} %get-tuple-element.8.gp, f32[16,512]{1,0:T(8,128)S(1)} %get-tuple-element.9.gphi, bf16[1,4096,256]{2,1,0:T(8,128)(2,1)S(1)} %get-tuple-element.10.gwi, ...), custom_call_target="tpu_custom_call" | custom-call | tf_op jit(solution)/shard_map/pallas_call | solution.py:534

commit v7 on v6

--- a/solution.py
+++ b/solution.py
@@ -50,14 +50,6 @@
     first = value.astype(BF16).astype(F32)
     second = (value - first).astype(BF16).astype(F32)
     return first, second, value - first - second
-
-
-def spread(column):
-    first, second, third = thirds(column)
-    lane = iota((8, LANE), 1)
-    return jnp.where(
-        lane == 0, first, jnp.where(lane == 1, second, jnp.where(lane == 2, third, 0.0))
-    )
 
 
 def kernel(
@@ -77,6 +69,9 @@
     def at_offset(dy, dx, dc):
         return (lax.rem(y + dy, 4) * 4 + lax.rem(x + dx, 4)) * 2 + lax.rem(core + dc, 2)
 
+    def along(d):
+        return lax.rem(z + jnp.where(core == 0, d, NZ - d), NZ)
+
     loads = [
         pltpu.make_async_copy(src, dst, in_sem.at[k])
         for k, (src, dst) in enumerate(
@@ -156,15 +151,13 @@
     pl.semaphore_wait(barrier, NZ - 1 + 7)
 
     for d in ALONG_EXP:
-        zz = lax.rem(z + d, NZ)
+        zz = along(d)
         remote(asend.at[zz], arecv.at[z], 0, r, zz).start()
 
     arecv[z] = asend[z]
     tell([sibling], 0)
     pl.semaphore_wait(known.at[0], 1)
     tell(x_line, 1)
-    loads[4].wait()
-    wot[...] = wov[0].T
     arrived(arecv.at[pl.ds(0, NZ - 1)], 0)
     total = arecv[0]
     for k in range(1, NZ):
@@ -172,13 +165,11 @@
     logit[z] = total
 
     for d in ALONG_EXP:
-        zz = lax.rem(z + d, NZ)
+        zz = along(d)
         remote(logit.at[z], logit.at[z], 1, r, zz).start()
 
     pl.semaphore_wait(known.at[1], 3)
     tell(y_line, 2)
-    loads[5].wait()
-    wit[...] = wiv[0].T
     loads[3].wait()
     arrived(logit.at[pl.ds(0, NZ - 1)], 1)
     pl.semaphore_wait(known.at[2], 3)
@@ -221,9 +212,10 @@
         return csend.at[pl.ds(pl.multiple_of(row * 16, 16), 16)]
 
     scatter(piece, crecv.at[pl.ds(pl.multiple_of(r * 16, 16), 16)], 2)
-    for i in range(2):
-        pvt[i] = pv[i].T
-        gvt[i] = gv[i].T
+    loads[4].wait()
+    wot[...] = wov[0].T
+    loads[5].wait()
+    wit[...] = wiv[0].T
     arrived(crecv, 2)
     cfull[...] = crecv[...].astype(F32)
     peak_all = cfull[pl.ds(12, 32, stride=16), :]
@@ -310,11 +302,15 @@
     pre_lo = jnp.concatenate([pre, none], axis=0).astype(BF16)
     result = (nn(active_lo, wov[0]) + nn(pre_lo, wit[...]))[0:8]
     wide = iota((8, 4096), 0) < 4
-    dots = jnp.sum(result * (rows_f[0:8, :] + rows_f[16:24, :]), axis=1, keepdims=True)
+    product = result * (rows_f[0:8, :] + rows_f[16:24, :])
+    dots = product[:, 0:LANE]
+    for k in range(1, 32):
+        dots = dots + product[:, k * LANE : (k + 1) * LANE]
+    dots_high = dots.astype(BF16).astype(F32)
     high = result.astype(BF16).astype(F32)
     rest = pltpu.roll(result - high, 4, 0)
     esend[...] = jnp.concatenate(
-        [high, jnp.where(wide, rest, jnp.concatenate([spread(dots)] * 32, axis=1))], axis=0
+        [high, jnp.where(wide, rest, jnp.concatenate([dots_high, dots - dots_high] * 16, axis=1))], axis=0
     ).astype(BF16)
 
     def block(qq, e):
@@ -324,6 +320,9 @@
 
     grad_w_out[0] = tn(active_hi, lhs).astype(BF16)
     grad_w_in[0] = tn(lhs, pre_lo).astype(BF16)
+    for i in range(2):
+        pvt[i] = pv[i].T
+        gvt[i] = gv[i].T
 
     arrived(erecv, 4)
     total = erecv[0].astype(F32)
@@ -331,9 +330,9 @@
         total = total + erecv[k].astype(F32)
     lower = iota((8, LANE), 0) < 4
     rest = pltpu.roll(total[8:16], 4, 0)
-    dots = spread(jnp.sum(rest, axis=1, keepdims=True))
+    high = rest.astype(BF16).astype(F32)
     fsend[...] = jnp.concatenate(
-        [jnp.where(lower, total[0:8], total[0:8] + rest), jnp.where(lower, dots, 0.0)], axis=0
+        [jnp.where(lower, total[0:8], total[0:8] + rest), jnp.where(lower, high, pltpu.roll(rest - high, 4, 0))], axis=0
     ).astype(BF16)
 
     frows = pl.ds(pl.multiple_of(source * 16, 16), 16)
@@ -348,13 +347,13 @@
     kind, slot = at // 32, lax.rem(at, 16)
     want = (slot // 2) * 16 + kind * 4 + (lax.rem(at, 32) // 16) * 2 + lax.rem(slot, 2)
     col = iota((96, LANE), 1)
-    pick = jnp.where(col == want, 1.0, 0.0).astype(BF16)
+    again = (kind == 2) & (col == want + 4)
+    pick = jnp.where((col == want) | again, 1.0, 0.0).astype(BF16)
 
     arrived(fwait, 5)
-    picked = nn(pick, frecv[...])
+    picked = nn(pick[0:64], frecv[...])
     slot_out = picked[0:32].astype(BF16)
     input_grad = picked[32:64].astype(BF16)
-    dots_b[...] = jnp.broadcast_to(jnp.sum(picked[64:96, 0:LANE], axis=1, keepdims=True), (32, LANE))
     for i in range(2):
         rows = slice(i * 16, i * 16 + 16)
         comb_part = nn(slot_out[rows], gvt[i])
@@ -365,10 +364,12 @@
             gsend[i * 4 + b, 16:32] = disp_part[:, lanes].astype(BF16)
 
     for d in ALONG_EXP:
-        zz = lax.rem(z + d, NZ)
+        zz = along(d)
         remote(gsend.at[zz], grecv.at[z], 6, r, zz).start()
 
     grecv[z] = gsend[z]
+    dots = jnp.sum(nn(pick[64:96], frecv[:, 0 : 2 * LANE]), axis=1, keepdims=True)
+    dots_b[...] = jnp.broadcast_to(dots, (32, LANE))
     chunk = logit[z]
     ec = jnp.exp(chunk - jnp.max(chunk, axis=0, keepdims=True))
     combine = ec / jnp.sum(ec, axis=0, keepdims=True)
@@ -384,7 +385,7 @@
     hbuf[z] = (combine * (comb_grad - row_dots) + dispatch * (disp_grad - col_dots)).astype(BF16)
 
     for d in ALONG_EXP:
-        zz = lax.rem(z + d, NZ)
+        zz = along(d)
         remote(hbuf.at[z], hbuf.at[z], 7, r, zz).start()
 
     dispatch_b = []

time: 66.4 us -> 66.2 us (level)
  no operation moved by 1% of the time
where the time goes in v7:
time: 66.2 us; the launch traced here: 66 us
  Pallas kernels  65.4 us (99%)
    pallas_call x1, Pallas kernels, local(): pl.pallas_call(kernel, out_shape=shapes, in_specs=[hbm] * 5, out_specs=[p...  63 us
    pallas_call x1, Pallas kernels, local(): pl.pallas_call(store_kernel, out_shape=shapes, in_specs=[anywhere] * 4, o...  2.44 us

profile of v7, /device:TPU:1, one launch (start us, length us, event | category | flops | bytes accessed | tf_op | source)
XLA Modules:
  0.0 66.0 jit_solution(9591777099769654621)
XLA Ops:
  0.6 63.0 %shard_map.84 = (bf16[2,512,512]{2,1,0:T(8,128)(2,1)S(1)}, f32[16,512]{1,0:T(8,128)S(1)}, bf16[1,4096,256]{2,1,0:T(8,128)(2,1)S(1)}, bf16[1,256,4096]{2,1,0:T(8,128)(2,1)S(1)}) custom-call(bf16[2,512,512]{2,1,0:T(8,128)(2,1)} %patches.1, bf16[2,512,512]{2,1,0:T(8,128)(2,1)} %grad_out.1, bf16[16,512]{1,0:T(8,128)(2,1)} %phi_t.1, bf16[1,4096,256]{2,1,0:T(8,128)(2,1)} %w_in.1, ...), custom_call_target="tpu_custom_call" | custom-call | flops 400000000 | bytes 12000000 | tf_op jit(solution)/shard_map/pallas_call | solution.py:483
  63.6 2.4 %shard_map.85 = (bf16[2,512,512]{2,1,0:T(8,128)(2,1)}, f32[16,512]{1,0:T(8,128)}, bf16[1,4096,256]{2,1,0:T(8,128)(2,1)}, bf16[1,256,4096]{2,1,0:T(8,128)(2,1)}) custom-call(bf16[2,512,512]{2,1,0:T(8,128)(2,1)S(1)} %get-tuple-element.8.gp, f32[16,512]{1,0:T(8,128)S(1)} %get-tuple-element.9.gphi, bf16[1,4096,256]{2,1,0:T(8,128)(2,1)S(1)} %get-tuple-element.10.gwi, ...), custom_call_target="tpu_custom_call" | custom-call | tf_op jit(solution)/shard_map/pallas_call | solution.py:535

commit v8 on v7

--- a/solution.py
+++ b/solution.py
@@ -412,7 +412,7 @@
     trade.wait_recv()
     half_sum = pair[core] + paired[...]
     isend[...] = half_sum.astype(BF16)
-    for dy, dx in CHIPS[:-1]:
+    for dy, dx in CHIPS[-2::-1]:
         remote(isend, irecv.at[r // 2], 9, at_offset(dy, dx, 0), z).start()
     irecv[r // 2] = isend[...]
     spread_patches(1)
@@ -450,10 +450,10 @@
 
 def store_kernel(gp, gphi, gwi, gwo, gp_out, gphi_out, gwi_out, gwo_out, sem):
     pieces = [(gphi, gphi_out)]
-    for k in range(4):
-        rows = pl.ds(k * 1024, 1024)
+    for k in range(2):
+        rows = pl.ds(k * 2048, 2048)
         pieces.append((gwi.at[:, rows], gwi_out.at[:, rows]))
-        rows = pl.ds(k * 64, 64)
+        rows = pl.ds(k * 128, 128)
         pieces.append((gwo.at[:, rows], gwo_out.at[:, rows]))
     for k in range(2):
         pieces.append((gp.at[k], gp_out.at[k]))
@@ -537,7 +537,7 @@
         out_shape=shapes,
         in_specs=[anywhere] * 4,
         out_specs=[hbm] * 4,
-        scratch_shapes=[pltpu.SemaphoreType.DMA((11,))],
+        scratch_shapes=[pltpu.SemaphoreType.DMA((7,))],
         compiler_params=pltpu.CompilerParams(vmem_limit_bytes=4 * 1024 * 1024),
     )(*held(results, pltpu.VMEM))
 

time: 66.2 us -> 66.9 us (1.011)
  Pallas kernels: 65.4 us -> 66.1 us
    pallas_call x1, Pallas kernels: 63 us -> 63.7 us  [local(): pl.pallas_call(kernel, out_shape=shapes, in_specs=[hbm] * 5, out_specs=[p...]
where the time goes in v8:
time: 66.9 us; the launch traced here: 66.7 us
  Pallas kernels  66.1 us (99%)
    pallas_call x1, Pallas kernels, local(): pl.pallas_call(kernel, out_shape=shapes, in_specs=[hbm] * 5, out_specs=[p...  63.7 us
    pallas_call x1, Pallas kernels, local(): pl.pallas_call(store_kernel, out_shape=shapes, in_specs=[anywhere] * 4, o...  2.41 us

profile of v8, /device:TPU:1, one launch (start us, length us, event | category | flops | bytes accessed | tf_op | source)
XLA Modules:
  0.0 66.7 jit_solution(5468136181204071434)
XLA Ops:
  0.6 63.7 %shard_map.84 = (bf16[2,512,512]{2,1,0:T(8,128)(2,1)S(1)}, f32[16,512]{1,0:T(8,128)S(1)}, bf16[1,4096,256]{2,1,0:T(8,128)(2,1)S(1)}, bf16[1,256,4096]{2,1,0:T(8,128)(2,1)S(1)}) custom-call(bf16[2,512,512]{2,1,0:T(8,128)(2,1)} %patches.1, bf16[2,512,512]{2,1,0:T(8,128)(2,1)} %grad_out.1, bf16[16,512]{1,0:T(8,128)(2,1)} %phi_t.1, bf16[1,4096,256]{2,1,0:T(8,128)(2,1)} %w_in.1, ...), custom_call_target="tpu_custom_call" | custom-call | flops 400000000 | bytes 12000000 | tf_op jit(solution)/shard_map/pallas_call | solution.py:483
  64.3 2.4 %shard_map.85 = (bf16[2,512,512]{2,1,0:T(8,128)(2,1)}, f32[16,512]{1,0:T(8,128)}, bf16[1,4096,256]{2,1,0:T(8,128)(2,1)}, bf16[1,256,4096]{2,1,0:T(8,128)(2,1)}) custom-call(bf16[2,512,512]{2,1,0:T(8,128)(2,1)S(1)} %get-tuple-element.8.gp, f32[16,512]{1,0:T(8,128)S(1)} %get-tuple-element.9.gphi, bf16[1,4096,256]{2,1,0:T(8,128)(2,1)S(1)} %get-tuple-element.10.gwi, ...), custom_call_target="tpu_custom_call" | custom-call | tf_op jit(solution)/shard_map/pallas_call | solution.py:535
